TPU v7x, 256 devices: a whole 4x4x8 slice. The times are simulated.
256 devices in a mesh: clip: 16 (over x, z_hi), seq: 16 (over y, z_lo, core).
Axes of the slice: x: 4, y: 4, z: 8 (z_hi: 4, z_lo: 2; z = z_hi * 2 + z_lo), core: 2. Of those that a mesh axis runs over, the one named last changes fastest.
Arguments:
- queries: bfloat16 [16, 2048, 3072], P('clip', 'seq'), may hold values from -6 to 6
- key_states: bfloat16 [16, 2048, 3072], P('clip', 'seq'), may hold values from -6 to 6
- value_states: bfloat16 [16, 2048, 3072], P('clip', 'seq'), may hold values from -6 to 6
- clip_lengths: int32 [16], replicated, may hold values from 512 to 2048, as said below
- tile_masks: int32 [16, 48, 16, 16], P('clip', 'seq'), may hold values from 0 to 1, as said below
Outputs:
- attended: bfloat16 [16, 2048, 3072], P('clip', 'seq')
Inputs may be any that keep to these rules, and one draw needn't show every extreme that they name: `clip_lengths`: every clip has at least 512 live tokens; some clip has exactly 2048. `tile_masks`: entries are 0 or 1; the diagonal tiles (i = j) are always 1.
All inputs are finite; a program needn't handle non-finite values.
Results may differ from a plain program's by a relative error of at most 0.0046.
Values may be sent and summed in bfloat16 or wider, within the bound.
No kernel may reach another device: no remote copies, remote signals or barrier semaphores. Data moves between devices by JAX's collectives and lax.ppermute only.
A program may use at most 64 MiB of HBM per device.

v0:
```python
import jax
import jax.numpy as jnp
from jax import lax
from jax.sharding import PartitionSpec as P

TILE = 128


def attend_head(query_head, key_head, value_head, mask_head, length):
    total_rows = query_head.shape[0]
    head_width = query_head.shape[1]
    block_rows = 4 * TILE
    score_scale = head_width ** (-0.5)
    positions = jnp.arange(total_rows, dtype=jnp.int32)
    key_live = positions < length

    def one_block(block_index, result):
        first_row = block_index * block_rows
        query_block = lax.dynamic_slice_in_dim(query_head, first_row, block_rows, 0)
        scores = (
            jnp.einsum("qd,kd->qk", query_block, key_head, preferred_element_type=jnp.float32)
            * score_scale
        )
        tile_rows = lax.dynamic_slice_in_dim(mask_head, block_index * 4, 4, 0)
        allowed = jnp.repeat(jnp.repeat(tile_rows, TILE, axis=0), TILE, axis=1) == 1
        allowed = allowed & key_live[None, :]
        scores = jnp.where(allowed, scores, -1e30)
        top_score = jnp.max(scores, axis=1, keepdims=True)
        weights = jnp.exp(scores - top_score)
        row_sums = jnp.sum(weights, axis=1, keepdims=True)
        rounded = weights.astype(jnp.bfloat16)
        mixed_rows = jnp.dot(rounded, value_head, preferred_element_type=jnp.float32) / row_sums
        row_live = first_row + jnp.arange(block_rows, dtype=jnp.int32) < length
        mixed_rows = jnp.where(row_live[:, None], mixed_rows, 0.0).astype(jnp.bfloat16)
        return lax.dynamic_update_slice_in_dim(result, mixed_rows, first_row, 0)

    block_count = (length + block_rows - 1) // block_rows
    initial = jnp.zeros((total_rows, head_width), jnp.bfloat16)
    return lax.fori_loop(jnp.int32(0), block_count, one_block, initial)


def on_device(queries, key_states, value_states, clip_lengths, tile_masks):
    head_queries, head_keys, head_values = (
        lax.all_to_all(queries[0], "seq", split_axis=1, concat_axis=0, tiled=True),
        lax.all_to_all(key_states[0], "seq", split_axis=1, concat_axis=0, tiled=True),
        lax.all_to_all(value_states[0], "seq", split_axis=1, concat_axis=0, tiled=True),
    )
    local_masks = tile_masks[0]
    heads_here = local_masks.shape[0]
    head_width = head_queries.shape[1] // heads_here
    clip_index = lax.axis_index("clip")
    own_length = lax.dynamic_index_in_dim(clip_lengths, clip_index, 0, False)

    def column(array, head):
        return array[:, head * head_width : (head + 1) * head_width]

    def local_head(head):
        return attend_head(
            column(head_queries, head),
            column(head_keys, head),
            column(head_values, head),
            local_masks[head],
            own_length,
        )

    outputs = [local_head(head) for head in range(heads_here)]
    joined = jnp.concatenate(outputs, axis=1)
    restored = lax.all_to_all(joined, "seq", split_axis=0, concat_axis=1, tiled=True)
    return restored[None]


def solution(mesh):
    in_specs = (
        P("clip", "seq", None),
        P("clip", "seq", None),
        P("clip", "seq", None),
        P(),
        P("clip", "seq", None, None),
    )
    out_specs = P("clip", "seq", None)
    return jax.shard_map(
        on_device, mesh=mesh, in_specs=in_specs, out_specs=out_specs, check_vma=False
    )
```

profile of v0, /device:TPU:163, one launch (start us, length us, event | category | flops | bytes accessed | tf_op | source)
XLA Modules:
  0.0 167.2 jit_solution(2187129390107892177)
XLA Ops:
  0.0 2.4 %copy.33 = bf16[1,128,3072]{1,2,0:T(8,128)(2,1)} copy(bf16[1,128,3072]{2,1,0:T(8,128)(2,1)} %param.12) | data formatting | bytes 1572864 | tf_op args[1]
  2.4 6.3 %all-to-all-start.1 = ((bf16[128,16,192]{0,2,1:T(8,128)(2,1)}), bf16[128,16,192]{0,2,1:T(8,128)(2,1)S(1)}, u32[]{:S(2)}, u32[]{:S(2)}) async-start(bf16[128,16,192]{0,2,1:T(8,128)(2,1)} %bitcast.4), calls=%async_computation.1 | async-start | bytes 1572864 | tf_op jit(solution)/shard_map/all_to_all | solution.py:45
  8.6 2.3 %copy.35 = bf16[1,128,3072]{1,2,0:T(8,128)(2,1)} copy(bf16[1,128,3072]{2,1,0:T(8,128)(2,1)} %param.13) | data formatting | bytes 1572864 | tf_op args[2]
  10.9 10.2 %all-to-all-done.1 = bf16[128,16,192]{0,2,1:T(8,128)(2,1)S(1)} async-done(((bf16[128,16,192]{0,2,1:T(8,128)(2,1)}), bf16[128,16,192]{0,2,1:T(8,128)(2,1)S(1)}, u32[]{:S(2)}, u32[]{:S(2)}) %all-to-all-start.1) | async-done | bytes 786464 | tf_op jit(solution)/shard_map/all_to_all | solution.py:45
  21.1 4.8 %all-to-all-start.2 = ((bf16[128,16,192]{0,2,1:T(8,128)(2,1)}), bf16[128,16,192]{0,2,1:T(8,128)(2,1)S(1)}, u32[]{:S(2)}, u32[]{:S(2)}) async-start(bf16[128,16,192]{0,2,1:T(8,128)(2,1)} %bitcast.6), calls=%async_computation.2 | async-start | bytes 1572864 | tf_op jit(solution)/shard_map/all_to_all | solution.py:46
  28.3 10.1 %all-to-all-done.2 = bf16[128,16,192]{0,2,1:T(8,128)(2,1)S(1)} async-done(((bf16[128,16,192]{0,2,1:T(8,128)(2,1)}), bf16[128,16,192]{0,2,1:T(8,128)(2,1)S(1)}, u32[]{:S(2)}, u32[]{:S(2)}) %all-to-all-start.2) | async-done | bytes 786464 | tf_op jit(solution)/shard_map/all_to_all | solution.py:46
  38.4 4.8 %all-to-all-start = ((bf16[128,16,192]{0,2,1:T(8,128)(2,1)}), bf16[128,16,192]{0,2,1:T(8,128)(2,1)S(1)}, u32[]{:S(2)}, u32[]{:S(2)}) async-start(bf16[128,16,192]{0,2,1:T(8,128)(2,1)} %bitcast.2), calls=%async_computation | async-start | bytes 1572864 | tf_op jit(solution)/shard_map/all_to_all | solution.py:44
  44.2 11.6 %all-to-all-done = bf16[128,16,192]{0,2,1:T(8,128)(2,1)S(1)} async-done(((bf16[128,16,192]{0,2,1:T(8,128)(2,1)}), bf16[128,16,192]{0,2,1:T(8,128)(2,1)S(1)}, u32[]{:S(2)}, u32[]{:S(2)}) %all-to-all-start) | async-done | bytes 786464 | tf_op jit(solution)/shard_map/all_to_all | solution.py:44
  56.0 30.7 %while.36 = (s32[]{:T(128)}, bf16[2048,64]{0,1:T(8,128)(2,1)S(1)}, s32[]{:T(128)}, s32[]{:T(128)}, s32[16,16]{1,0:T(8,128)S(1)}, /*index=5*/bf16[2048,64]{0,1:T(...) while((s32[]{:T(128)}, bf16[2048,64]{0,1:T(8,128)(2,1)S(1)}, ...), condition=%wide.region_3.4_spmd.clone.clone, body=%wide.region_0.3_spmd.clone.clone.sunk | while | flops 276924480 | bytes 15892089 | solution.py:39
  56.1 3.5 %broadcast_in_dim.126 = pred[512,16,128]{2,1,0:T(8,128)(4,1)S(1)} broadcast(pred[512,16]{1,0:T(8,128)(4,1)S(1)} %bitcast.87), dimensions={0,1} | broadcast | bytes 1056768 | tf_op jit(solution)/shard_map/while/body/broadcast_in_dim | solution.py:25
  63.7 3.5 %broadcast_in_dim.126 = pred[512,16,128]{2,1,0:T(8,128)(4,1)S(1)} broadcast(pred[512,16]{1,0:T(8,128)(4,1)S(1)} %bitcast.87), dimensions={0,1} | broadcast | bytes 1056768 | tf_op jit(solution)/shard_map/while/body/broadcast_in_dim | solution.py:25
  71.4 3.5 %broadcast_in_dim.126 = pred[512,16,128]{2,1,0:T(8,128)(4,1)S(1)} broadcast(pred[512,16]{1,0:T(8,128)(4,1)S(1)} %bitcast.87), dimensions={0,1} | broadcast | bytes 1056768 | tf_op jit(solution)/shard_map/while/body/broadcast_in_dim | solution.py:25
  79.1 3.5 %broadcast_in_dim.126 = pred[512,16,128]{2,1,0:T(8,128)(4,1)S(1)} broadcast(pred[512,16]{1,0:T(8,128)(4,1)S(1)} %bitcast.87), dimensions={0,1} | broadcast | bytes 1056768 | tf_op jit(solution)/shard_map/while/body/broadcast_in_dim | solution.py:25
  87.3 30.7 %while.37 = (s32[]{:T(128)}, bf16[2048,64]{0,1:T(8,128)(2,1)S(1)}, s32[]{:T(128)}, s32[]{:T(128)}, s32[16,16]{1,0:T(8,128)S(1)}, /*index=5*/bf16[2048,64]{0,1:T(...) while((s32[]{:T(128)}, bf16[2048,64]{0,1:T(8,128)(2,1)S(1)}, ...), condition=%wide.region_7.8_spmd.clone.clone, body=%wide.region_4.7_spmd.clone.clone.sunk | while | flops 276924480 | bytes 15892089 | solution.py:39
  87.4 3.5 %broadcast_in_dim.130 = pred[512,16,128]{2,1,0:T(8,128)(4,1)S(1)} broadcast(pred[512,16]{1,0:T(8,128)(4,1)S(1)} %bitcast.88), dimensions={0,1} | broadcast | bytes 1056768 | tf_op jit(solution)/shard_map/while/body/broadcast_in_dim | solution.py:25
  95.0 3.5 %broadcast_in_dim.130 = pred[512,16,128]{2,1,0:T(8,128)(4,1)S(1)} broadcast(pred[512,16]{1,0:T(8,128)(4,1)S(1)} %bitcast.88), dimensions={0,1} | broadcast | bytes 1056768 | tf_op jit(solution)/shard_map/while/body/broadcast_in_dim | solution.py:25
  102.7 3.5 %broadcast_in_dim.130 = pred[512,16,128]{2,1,0:T(8,128)(4,1)S(1)} broadcast(pred[512,16]{1,0:T(8,128)(4,1)S(1)} %bitcast.88), dimensions={0,1} | broadcast | bytes 1056768 | tf_op jit(solution)/shard_map/while/body/broadcast_in_dim | solution.py:25
  110.4 3.5 %broadcast_in_dim.130 = pred[512,16,128]{2,1,0:T(8,128)(4,1)S(1)} broadcast(pred[512,16]{1,0:T(8,128)(4,1)S(1)} %bitcast.88), dimensions={0,1} | broadcast | bytes 1056768 | tf_op jit(solution)/shard_map/while/body/broadcast_in_dim | solution.py:25
  118.6 30.9 %while.38 = (s32[]{:T(128)}, bf16[2048,64]{0,1:T(8,128)(2,1)S(1)}, s32[]{:T(128)}, s32[]{:T(128)}, s32[16,16]{1,0:T(8,128)S(1)}, /*index=5*/bf16[2048,64]{0,1:T(...) while((s32[]{:T(128)}, bf16[2048,64]{0,1:T(8,128)(2,1)S(1)}, ...), condition=%wide.region_11.12_spmd.clone.clone, body=%wide.region_8.11_spmd.clone.clone.sunk | while | flops 276924480 | bytes 15892089 | solution.py:39
  118.8 3.5 %broadcast_in_dim.134 = pred[512,16,128]{2,1,0:T(8,128)(4,1)S(1)} broadcast(pred[512,16]{1,0:T(8,128)(4,1)S(1)} %bitcast.89), dimensions={0,1} | broadcast | bytes 1056768 | tf_op jit(solution)/shard_map/while/body/broadcast_in_dim | solution.py:25
  126.5 3.5 %broadcast_in_dim.134 = pred[512,16,128]{2,1,0:T(8,128)(4,1)S(1)} broadcast(pred[512,16]{1,0:T(8,128)(4,1)S(1)} %bitcast.89), dimensions={0,1} | broadcast | bytes 1056768 | tf_op jit(solution)/shard_map/while/body/broadcast_in_dim | solution.py:25
  134.2 3.5 %broadcast_in_dim.134 = pred[512,16,128]{2,1,0:T(8,128)(4,1)S(1)} broadcast(pred[512,16]{1,0:T(8,128)(4,1)S(1)} %bitcast.89), dimensions={0,1} | broadcast | bytes 1056768 | tf_op jit(solution)/shard_map/while/body/broadcast_in_dim | solution.py:25
  141.8 3.5 %broadcast_in_dim.134 = pred[512,16,128]{2,1,0:T(8,128)(4,1)S(1)} broadcast(pred[512,16]{1,0:T(8,128)(4,1)S(1)} %bitcast.89), dimensions={0,1} | broadcast | bytes 1056768 | tf_op jit(solution)/shard_map/while/body/broadcast_in_dim | solution.py:25
  149.6 16.4 %all_to_all.73 = bf16[16,128,192]{1,2,0:T(8,128)(2,1)S(1)} all-to-all(bf16[16,128,192]{1,2,0:T(8,128)(2,1)S(1)} %copy_bitcast_fusion.3), channel_id=1, replica_groups=mesh['clip'=16,'seq'=16] {'seq'}, dimensions={0} | all-to-all | bytes 1572864 | tf_op jit(solution)/shard_map/all_to_all | solution.py:68
  (110 shorter events, 54.9 us)
Async XLA Ops:
  0.0 25.9 %copy-start.2 = (s32[16]{0:T(128)S(1)}, s32[16]{0:T(128)}, u32[]{:S(2)}) copy-start(s32[16]{0:T(128)} %param.14) | copy-start | bytes 196
  0.0 27.2 %copy-start = (bf16[1,128,3072]{2,1,0:T(8,128)(2,1)S(1)}, bf16[1,128,3072]{2,1,0:T(8,128)(2,1)}, u32[]{:S(2)}) copy-start(bf16[1,128,3072]{2,1,0:T(8,128)(2,1)} %param.11) | copy-start | bytes 2359300
  0.0 28.3 %copy-start.1 = (s32[1,3,16,16]{3,2,1,0:T(8,128)S(1)}, s32[1,3,16,16]{3,2,1,0:T(8,128)}, u32[]{:S(2)}) copy-start(s32[1,3,16,16]{3,2,1,0:T(8,128)} %param.15) | copy-start | bytes 9220
  2.4 18.8 %all-to-all-start.1 = ((bf16[128,16,192]{0,2,1:T(8,128)(2,1)}), bf16[128,16,192]{0,2,1:T(8,128)(2,1)S(1)}, u32[]{:S(2)}, u32[]{:S(2)}) async-start(bf16[128,16,192]{0,2,1:T(8,128)(2,1)} %bitcast.4), calls=%async_computation.1 | async-start | bytes 1572864 | tf_op jit(solution)/shard_map/all_to_all | solution.py:45
  21.1 17.3 %all-to-all-start.2 = ((bf16[128,16,192]{0,2,1:T(8,128)(2,1)}), bf16[128,16,192]{0,2,1:T(8,128)(2,1)S(1)}, u32[]{:S(2)}, u32[]{:S(2)}) async-start(bf16[128,16,192]{0,2,1:T(8,128)(2,1)} %bitcast.6), calls=%async_computation.2 | async-start | bytes 1572864 | tf_op jit(solution)/shard_map/all_to_all | solution.py:46
  38.4 17.3 %all-to-all-start = ((bf16[128,16,192]{0,2,1:T(8,128)(2,1)}), bf16[128,16,192]{0,2,1:T(8,128)(2,1)S(1)}, u32[]{:S(2)}, u32[]{:S(2)}) async-start(bf16[128,16,192]{0,2,1:T(8,128)(2,1)} %bitcast.2), calls=%async_computation | async-start | bytes 1572864 | tf_op jit(solution)/shard_map/all_to_all | solution.py:44
where the time goes:
time: 169 us; the launch traced here: 167 us
  local copies, waits for them, and re-layouts  51.7 us (31%)
  waiting for transfers between devices  32 us (19%)
  matrix products  25.2 us (15%)
  other arithmetic  24.3 us (14%)
  blocking collectives  16.4 us (10%)
  starting transfers between devices  15.8 us (9%)
    broadcast_in_dim x24, local copies, waits for them, and re-layouts, one_block(): allowed = jnp.repeat(jnp.repeat(tile_rows, TILE, axis=0), TILE, axis=1) == 1  41.9 us
    all_to_all x1, blocking collectives, on_device(): lax.all_to_all(joined, 'seq', split_axis=0, concat_axis=1, tiled=True)  16.4 us
    dot_general x12, matrix products, one_block(): jnp.einsum('qd,kd->qk', query_block, key_head, preferred_element_type=jnp...  14.6 us
    all_to_all x1, waiting for transfers between devices, on_device(): lax.all_to_all(queries[0], 'seq', split_axis=1, concat_axis=0, tiled=True)  11.6 us
    dot_general x12, matrix products, one_block(): jnp.dot(rounded, value_head, preferred_element_type=jnp.float32) / row_sums  10.6 us
    all_to_all x1, waiting for transfers between devices, on_device(): lax.all_to_all(key_states[0], 'seq', split_axis=1, concat_axis=0, tiled=T...  10.2 us
    all_to_all x1, waiting for transfers between devices, on_device(): lax.all_to_all(value_states[0], 'seq', split_axis=1, concat_axis=0, tiled...  10.1 us
    reduce_sum x12, other arithmetic, one_block(): row_sums = jnp.sum(weights, axis=1, keepdims=True)  8.53 us
  transfers between devices with their start and end apart: 3, of which 3 were waited for; matrix products, arithmetic and copies ran while one was open for 3% of the time, Pallas kernels for 0%

commit v1 on v0

v1 whole, which is shorter than its diff:
```python
import jax
import jax.numpy as jnp
from jax import lax
from jax.experimental import pallas as pl
from jax.experimental.pallas import tpu as pltpu
from jax.sharding import PartitionSpec as P

TILE = 128
SEQ = 16
CHIPS = 8
PAIR = 128
PAIRS = 3
QB = 256
CK = 256
NQ = CHIPS * TILE
NK = 2 * NQ
MASKED = -1e30
SCALE = 0.125 * 1.4426950408889634

ALL_CHIPS = [[2 * chip + core for chip in range(CHIPS)] for core in range(2)]
OTHER_CORE = [(device, device ^ 1) for device in range(SEQ)]


def matmul(a, b, dims):
    return lax.dot_general(a, b, (dims, ((), ())), preferred_element_type=jnp.float32)


def attend(core_ref, length_ref, q_ref, k_own, v_own, k_sib, v_sib, mask_ref, o_ref,
           key_aux, keys, values_t, scores_a, scores_b):
    core = core_ref[0]
    length = length_ref[0]
    lane = lax.broadcasted_iota(jnp.int32, (1, PAIR), 1)
    low = lane < 64
    scores = (scores_a, scores_b)

    @pl.when(pl.program_id(0) == 0)
    def _():
        column = lax.broadcasted_iota(jnp.int32, (TILE, PAIR), 1) & 63
        inside = lax.broadcasted_iota(jnp.int32, (TILE, PAIR), 0)
        for part in range(2):
            parity = core if part == 0 else 1 - core
            for chip in range(CHIPS):
                tile = 2 * chip + parity
                dead = jnp.where(tile * TILE + inside >= length, 16, -1)
                hot = (column == tile) | (column == dead)
                first = part * NQ + chip * TILE
                key_aux[first : first + TILE, :] = hot.astype(jnp.float32).astype(jnp.bfloat16)

    for part, (k_ref, v_ref) in enumerate(((k_own, v_own), (k_sib, v_sib))):
        for chip in range(CHIPS):
            rows = slice(part * NQ + chip * TILE, part * NQ + (chip + 1) * TILE)
            k = k_ref[chip, 0]
            keys[0, rows, :] = jnp.where(low, k, key_aux[rows, :])
            keys[1, rows, :] = jnp.where(low, key_aux[rows, :], k)
            values_t[:, rows] = v_ref[chip, 0].T

    def load_queries(block, head):
        parts = []
        for half in range(2):
            chip = 2 * block + half
            kept = mask_ref[head, pl.ds(2 * chip + core, 1), :]
            bias = jnp.where(kept == 1, 0.0, MASKED)
            bias = jnp.where((lane & 63) < 16, bias, jnp.where((lane & 63) == 16, MASKED, 0.0))
            bias = jnp.broadcast_to(bias, (TILE, PAIR)).astype(jnp.bfloat16)
            q = q_ref[chip, 0]
            parts.append(jnp.where(low, q, bias) if head == 0 else jnp.where(low, bias, q))
        return jnp.concatenate(parts, axis=0)

    def score_chunk(chunk, queries, head, top):
        rows = slice(chunk * CK, (chunk + 1) * CK)
        s = matmul(keys[head, rows, :], queries, ((1,), (1,)))
        scores[head][rows, :] = s
        return jnp.maximum(top, jnp.max(s.reshape(CK // 8, 8, QB), axis=0))

    empty = jnp.full((8, QB), -3e38, jnp.float32)

    def step(block, head, top, next_block):
        queries = load_queries(next_block, 1 - head)
        next_top = empty
        total = jnp.zeros((8, QB), jnp.float32)
        mixed = jnp.zeros((64, QB), jnp.float32)
        row_top = jnp.max(top, axis=0, keepdims=True)
        for chunk in range(NK // CK):
            next_top = score_chunk(chunk, queries, 1 - head, next_top)
            rows = slice(chunk * CK, (chunk + 1) * CK)
            weights = jnp.exp2((scores[head][rows, :] - row_top) * SCALE)
            total = total + jnp.sum(weights.reshape(CK // 8, 8, QB), axis=0)
            mixed = mixed + matmul(
                values_t[64 * head : 64 * head + 64, rows], weights.astype(jnp.bfloat16), ((1,), (0,))
            )
        return next_top, mixed / jnp.sum(total, axis=0, keepdims=True)

    top = empty
    queries = load_queries(0, 0)
    for chunk in range(NK // CK):
        top = score_chunk(chunk, queries, 0, top)

    blocks = NQ // QB
    query = lax.broadcasted_iota(jnp.int32, (1, QB), 1)

    def body(block, top):
        top, first = step(block, 0, top, block)
        top, second = step(block, 1, top, jnp.minimum(block + 1, blocks - 1))
        chip = 2 * block + query // TILE
        live = (2 * chip + core) * TILE + query % TILE < length
        both = jnp.where(live, jnp.concatenate([first, second], axis=0), 0.0).T.astype(jnp.bfloat16)
        o_ref[2 * block] = both[:TILE]
        o_ref[2 * block + 1] = both[TILE:]
        return top

    lax.fori_loop(0, blocks, body, top)


def attention(core, length, own, sibling, masks):
    def tokens(which):
        return pl.BlockSpec((CHIPS, 1, TILE, PAIR), lambda pair: (0, which, 0, pair))

    return pl.pallas_call(
        attend,
        grid=(PAIRS,),
        out_shape=jax.ShapeDtypeStruct((CHIPS, TILE, PAIRS * PAIR), jnp.bfloat16),
        in_specs=[
            pl.BlockSpec(memory_space=pltpu.SMEM),
            pl.BlockSpec(memory_space=pltpu.SMEM),
            tokens(0), tokens(1), tokens(2), tokens(1), tokens(2),
            pl.BlockSpec((2, 16, PAIR), lambda pair: (pair, 0, 0)),
        ],
        out_specs=pl.BlockSpec((CHIPS, TILE, PAIR), lambda pair: (0, 0, pair)),
        scratch_shapes=[
            pltpu.VMEM((NK, PAIR), jnp.bfloat16),
            pltpu.VMEM((2, NK, PAIR), jnp.bfloat16),
            pltpu.VMEM((PAIR, NK), jnp.bfloat16),
            pltpu.VMEM((NK, QB), jnp.float32),
            pltpu.VMEM((NK, QB), jnp.float32),
        ],
        compiler_params=pltpu.CompilerParams(vmem_limit_bytes=40 * 2**20),
        cost_estimate=pl.CostEstimate(
            flops=4 * 6 * NQ * NK * 64, bytes_accessed=8 * 2**20, transcendentals=6 * NQ * NK
        ),
    )(core, length, own, own, own, sibling, sibling, masks)


def split_columns(*refs):
    *arrays, packed, done = refs
    copies = []
    for chip in range(CHIPS):
        for which, array in enumerate(arrays):
            columns = array.at[0, :, pl.ds(chip * PAIRS * PAIR, PAIRS * PAIR)]
            copies.append(pltpu.make_async_copy(columns, packed.at[chip, which], done.at[len(copies)]))
    for copy in copies:
        copy.start()
    for copy in copies:
        copy.wait()


def join_columns(blocks, rows, done):
    copies = [
        pltpu.make_async_copy(
            blocks.at[chip], rows.at[0, :, pl.ds(chip * PAIRS * PAIR, PAIRS * PAIR)], done.at[chip]
        )
        for chip in range(CHIPS)
    ]
    for copy in copies:
        copy.start()
    for copy in copies:
        copy.wait()


def move(kernel, shape, copies, *arrays):
    whole = pl.BlockSpec(memory_space=pl.ANY)
    return pl.pallas_call(
        kernel,
        out_shape=jax.ShapeDtypeStruct(shape, jnp.bfloat16),
        in_specs=[whole] * len(arrays),
        out_specs=whole,
        scratch_shapes=[pltpu.SemaphoreType.DMA((copies,))],
    )(*arrays)


def on_device(queries, key_states, value_states, clip_lengths, tile_masks):
    place = lax.axis_index("seq")
    core = place % 2
    length = lax.dynamic_slice_in_dim(clip_lengths, lax.axis_index("clip"), 1, 0)

    mine = jnp.pad(tile_masks[0], ((0, 0), (0, 0), (0, 48)))
    mine = jnp.concatenate([mine, mine], axis=-1)
    other = lax.ppermute(mine, "seq", OTHER_CORE)
    masks = jnp.where(core == 0, jnp.concatenate([mine, other]), jnp.concatenate([other, mine]))

    packed = move(
        split_columns, (CHIPS, 3, TILE, PAIRS * PAIR), 3 * CHIPS, queries, key_states, value_states
    )
    own = lax.all_to_all(packed, "seq", 0, 0, tiled=True, axis_index_groups=ALL_CHIPS)
    sibling = lax.ppermute(own, "seq", OTHER_CORE)
    mixed = attention(core.reshape(1), length, own, sibling, masks)
    back = lax.all_to_all(mixed, "seq", 0, 0, tiled=True, axis_index_groups=ALL_CHIPS)
    return move(join_columns, (1, TILE, CHIPS * PAIRS * PAIR), CHIPS, back)


def solution(mesh):
    split = P("clip", "seq", None)
    return jax.shard_map(
        on_device,
        mesh=mesh,
        in_specs=(split, split, split, P(), P("clip", "seq", None, None)),
        out_specs=split,
        check_vma=False,
    )
```

time: 169 us -> 175 us (1.036)
  the two profiles are of different devices: /device:TPU:163 before, /device:TPU:1 now
where the time goes in v1:
time: 175 us
  Pallas kernels  117 us (67%)
  blocking collectives  51.3 us (29%)
  waiting for transfers between devices  3.43 us (2%)
  starting transfers between devices  1.9 us (1%)
    pallas_call x2, Pallas kernels, move(): pl.pallas_call(kernel, out_shape=jax.ShapeDtypeStruct(shape, jnp.bfloat16...  97.8 us
    all_to_all x1, blocking collectives, on_device(): lax.all_to_all(packed, 'seq', 0, 0, tiled=True, axis_index_groups=ALL_CHIPS)  35.6 us
    pallas_call x1, Pallas kernels, attention(): pl.pallas_call(attend, grid=(PAIRS,), out_shape=jax.ShapeDtypeStruct((CHI...  19.5 us
    all_to_all x1, blocking collectives, on_device(): lax.all_to_all(mixed, 'seq', 0, 0, tiled=True, axis_index_groups=ALL_CHIPS)  15.7 us
  transfers between devices with their start and end apart: 2, of which 2 were waited for; matrix products, arithmetic and copies ran while one was open for 0% of the time, Pallas kernels for 0%

profile of v1, /device:TPU:1, one launch (start us, length us, event | category | flops | bytes accessed | tf_op | source)
XLA Modules:
  0.0 174.8 jit_solution(14251047136665944390)
XLA Ops:
  0.0 72.8 %shard_map.55 = bf16[8,3,128,384]{3,2,1,0:T(8,128)(2,1)} custom-call(bf16[1,128,3072]{2,1,0:T(8,128)(2,1)} %refs_0_.1, bf16[1,128,3072]{2,1,0:T(8,128)(2,1)} %refs_1_.1, bf16[1,128,3072]{2,1,0:T(8,128)(2,1)} %refs_2_.1), custom_call_target="tpu_custom_call" | custom-call | tf_op jit(solution)/shard_map/pallas_call | solution.py:171
  72.8 0.0 copy-start
  72.8 0.0 copy-start.1
  72.8 35.6 %all_to_all.10.q_ref.k_own.v_own = bf16[8,3,128,384]{3,2,1,0:T(8,128)(2,1)S(1)} all-to-all(bf16[8,3,128,384]{3,2,1,0:T(8,128)(2,1)} %shard_map.55), channel_id=1, replica_groups={{0,2,4,6,8,10,12,14},{1,3,5,7,9,11,13,15},{16,18,20,22,24,26,28,30},{17..., dimensions={0} | all-to-all | bytes 4718592 | tf_op jit(solution)/shard_map/all_to_all | solution.py:193
  108.4 1.9 %collective-permute-start = (bf16[8,3,128,384]{3,2,1,0:T(8,128)(2,1)S(1)}, bf16[8,3,128,384]{3,2,1,0:T(8,128)(2,1)}, u32[]{:S(2)}, u32[]{:S(2)}) collective-permute-start(bf16[8,3,128,384]{3,2,1,0:T(8,128)(2,1)S(1)} %all_to_all.10.q_ref.k_own.v_own), channel_id=1, source_target_pairs={{0,1},{1,0},{2,3},{3,2},{4,5},{5,4},{6,7},{7,6},{8,9},{9,8},{10,11... | collective-permute-start | bytes 7077896 | tf_op jit(solution)/shard_map/ppermute | solution.py:194
  110.2 0.0 copy-done
  110.3 0.1 pad_add_fusion
  110.3 0.0 collective-permute-start.1
  110.4 0.0 copy-done.1
  110.4 0.7 dynamic_slice.3.length_ref
  111.1 3.3 %collective-permute-done.1 = s32[3,16,128]{2,1,0:T(8,128)S(1)} collective-permute-done((s32[3,16,128]{2,1,0:T(8,128)S(1)}, s32[3,16,128]{2,1,0:T(8,128)S(1)}, u32[]{:S(2)}, u32[]{:S(2)}) %collective-permute-start.1) | collective-permute-done | bytes 24608 | tf_op jit(solution)/shard_map/ppermute | solution.py:187
  114.3 0.1 add_select_fusion.mask_ref
  114.4 0.2 collective-permute-done.k_sib.v_sib
  114.6 19.5 %shard_map.56 = bf16[8,128,384]{2,1,0:T(8,128)(2,1)S(1)} custom-call(s32[1]{0:T(128)} %bitcast.core_ref, s32[1]{0:T(128)} %dynamic_slice.3.length_ref, bf16[8,3,128,384]{3,2,1,0:T(8,128)(2,1)S(1)} %all_to_all.10.q_ref.k_own.v_own, bf16[8,3,128,384]{3,2,1,0:T(8,128)(2,1)S(1)} %all_to_all.10.q_ref.k_own.v_own, ...), custom_call_target="tpu_custom_call" | custom-call | flops 3221225472 | bytes 8388608 | tf_op jit(solution)/shard_map/pallas_call | solution.py:118
  134.1 15.7 %all_to_all.11.blocks = bf16[8,128,384]{2,1,0:T(8,128)(2,1)} all-to-all(bf16[8,128,384]{2,1,0:T(8,128)(2,1)S(1)} %shard_map.56), channel_id=1, replica_groups={{0,2,4,6,8,10,12,14},{1,3,5,7,9,11,13,15},{16,18,20,22,24,26,28,30},{17..., dimensions={0} | all-to-all | bytes 1572864 | tf_op jit(solution)/shard_map/all_to_all | solution.py:196
  149.8 25.0 %shard_map.57 = bf16[1,128,3072]{2,1,0:T(8,128)(2,1)} custom-call(bf16[8,128,384]{2,1,0:T(8,128)(2,1)} %all_to_all.11.blocks), custom_call_target="tpu_custom_call" | custom-call | tf_op jit(solution)/shard_map/pallas_call | solution.py:171
  (1 shorter events, 0.0 us)
Async XLA Ops:
  72.8 37.5 %copy-start = (s32[1,3,16,16]{3,2,1,0:T(8,128)S(1)}, s32[1,3,16,16]{3,2,1,0:T(8,128)}, u32[]{:S(2)}) copy-start(s32[1,3,16,16]{3,2,1,0:T(8,128)} %param.9) | copy-start | bytes 9220
  72.8 37.6 %copy-start.1 = (s32[16]{0:T(128)S(1)}, s32[16]{0:T(128)}, u32[]{:S(2)}) copy-start(s32[16]{0:T(128)} %param.8) | copy-start | bytes 196
  108.4 6.2 %collective-permute-start = (bf16[8,3,128,384]{3,2,1,0:T(8,128)(2,1)S(1)}, bf16[8,3,128,384]{3,2,1,0:T(8,128)(2,1)}, u32[]{:S(2)}, u32[]{:S(2)}) collective-permute-start(bf16[8,3,128,384]{3,2,1,0:T(8,128)(2,1)S(1)} %all_to_all.10.q_ref.k_own.v_own), channel_id=1, source_target_pairs={{0,1},{1,0},{2,3},{3,2},{4,5},{5,4},{6,7},{7,6},{8,9},{9,8},{10,11... | collective-permute-start | bytes 7077896 | tf_op jit(solution)/shard_map/ppermute | solution.py:194
  110.3 4.0 %collective-permute-start.1 = (s32[3,16,128]{2,1,0:T(8,128)S(1)}, s32[3,16,128]{2,1,0:T(8,128)S(1)}, u32[]{:S(2)}, u32[]{:S(2)}) collective-permute-start(s32[3,16,128]{2,1,0:T(8,128)S(1)} %pad_add_fusion), channel_id=1, source_target_pairs={{0,1},{1,0},{2,3},{3,2},{4,5},{5,4},{6,7},{7,6},{8,9},{9,8},{10,11... | collective-permute-start | bytes 73736 | tf_op jit(solution)/shard_map/ppermute | solution.py:187

commit v2 on v1

--- a/solution.py
+++ b/solution.py
@@ -140,41 +140,35 @@
     )(core, length, own, own, own, sibling, sibling, masks)
 
 
-def split_columns(*refs):
-    *arrays, packed, done = refs
-    copies = []
-    for chip in range(CHIPS):
-        for which, array in enumerate(arrays):
-            columns = array.at[0, :, pl.ds(chip * PAIRS * PAIR, PAIRS * PAIR)]
-            copies.append(pltpu.make_async_copy(columns, packed.at[chip, which], done.at[len(copies)]))
-    for copy in copies:
-        copy.start()
-    for copy in copies:
-        copy.wait()
-
-
-def join_columns(blocks, rows, done):
-    copies = [
-        pltpu.make_async_copy(
-            blocks.at[chip], rows.at[0, :, pl.ds(chip * PAIRS * PAIR, PAIRS * PAIR)], done.at[chip]
-        )
-        for chip in range(CHIPS)
-    ]
-    for copy in copies:
-        copy.start()
-    for copy in copies:
-        copy.wait()
-
-
-def move(kernel, shape, copies, *arrays):
-    whole = pl.BlockSpec(memory_space=pl.ANY)
+def split_kernel(q_ref, k_ref, v_ref, packed_ref):
+    packed_ref[0, 0] = q_ref[0]
+    packed_ref[0, 1] = k_ref[0]
+    packed_ref[0, 2] = v_ref[0]
+
+
+def split_columns(*arrays):
+    columns = pl.BlockSpec((1, TILE, PAIRS * PAIR), lambda chip: (0, 0, chip))
     return pl.pallas_call(
-        kernel,
-        out_shape=jax.ShapeDtypeStruct(shape, jnp.bfloat16),
-        in_specs=[whole] * len(arrays),
-        out_specs=whole,
-        scratch_shapes=[pltpu.SemaphoreType.DMA((copies,))],
+        split_kernel,
+        grid=(CHIPS,),
+        out_shape=jax.ShapeDtypeStruct((CHIPS, 3, TILE, PAIRS * PAIR), jnp.bfloat16),
+        in_specs=[columns] * 3,
+        out_specs=pl.BlockSpec((1, 3, TILE, PAIRS * PAIR), lambda chip: (chip, 0, 0, 0)),
     )(*arrays)
+
+
+def join_kernel(block_ref, rows_ref):
+    rows_ref[...] = block_ref[...]
+
+
+def join_columns(blocks):
+    return pl.pallas_call(
+        join_kernel,
+        grid=(CHIPS,),
+        out_shape=jax.ShapeDtypeStruct((1, TILE, CHIPS * PAIRS * PAIR), jnp.bfloat16),
+        in_specs=[pl.BlockSpec((1, TILE, PAIRS * PAIR), lambda chip: (chip, 0, 0))],
+        out_specs=pl.BlockSpec((1, TILE, PAIRS * PAIR), lambda chip: (0, 0, chip)),
+    )(blocks)
 
 
 def on_device(queries, key_states, value_states, clip_lengths, tile_masks):
@@ -187,14 +181,12 @@
     other = lax.ppermute(mine, "seq", OTHER_CORE)
     masks = jnp.where(core == 0, jnp.concatenate([mine, other]), jnp.concatenate([other, mine]))
 
-    packed = move(
-        split_columns, (CHIPS, 3, TILE, PAIRS * PAIR), 3 * CHIPS, queries, key_states, value_states
-    )
+    packed = split_columns(queries, key_states, value_states)
     own = lax.all_to_all(packed, "seq", 0, 0, tiled=True, axis_index_groups=ALL_CHIPS)
     sibling = lax.ppermute(own, "seq", OTHER_CORE)
     mixed = attention(core.reshape(1), length, own, sibling, masks)
     back = lax.all_to_all(mixed, "seq", 0, 0, tiled=True, axis_index_groups=ALL_CHIPS)
-    return move(join_columns, (1, TILE, CHIPS * PAIRS * PAIR), CHIPS, back)
+    return join_columns(back)
 
 
 def solution(mesh):

time: 175 us -> 88.8 us (0.51)
  Pallas kernels: 117 us -> 30.5 us
    pallas_call x2, Pallas kernels: 97.8 us -> 11 us  [the longest x1 5.98 us: split_columns(): pl.pallas_call(split_kernel, grid=(CHIPS,), out_shape=jax.ShapeDtypeStruc...]
  transfers between devices with their start and end apart: 2 -> 2, of which waited for: 2 -> 2; matrix products, arithmetic and copies ran while one was open for 0% -> 1% of each run, Pallas kernels for 0% -> 0%
where the time goes in v2:
time: 88.8 us; the launch traced here: 88.2 us
  blocking collectives  51.4 us (58%)
  Pallas kernels  30.5 us (34%)
  waiting for transfers between devices  3.43 us (4%)
  starting transfers between devices  1.9 us (2%)
    all_to_all x1, blocking collectives, on_device(): lax.all_to_all(packed, 'seq', 0, 0, tiled=True, axis_index_groups=ALL_CHIPS)  35.7 us
    pallas_call x1, Pallas kernels, attention(): pl.pallas_call(attend, grid=(PAIRS,), out_shape=jax.ShapeDtypeStruct((CHI...  19.5 us
    all_to_all x1, blocking collectives, on_device(): lax.all_to_all(mixed, 'seq', 0, 0, tiled=True, axis_index_groups=ALL_CHIPS)  15.7 us
    pallas_call x1, Pallas kernels, split_columns(): pl.pallas_call(split_kernel, grid=(CHIPS,), out_shape=jax.ShapeDtypeStruc...  5.98 us
    pallas_call x1, Pallas kernels, join_columns(): pl.pallas_call(join_kernel, grid=(CHIPS,), out_shape=jax.ShapeDtypeStruct...  5.04 us
    ppermute x1, waiting for transfers between devices, on_device(): other = lax.ppermute(mine, 'seq', OTHER_CORE)  3.25 us
    ppermute x1, starting transfers between devices, on_device(): sibling = lax.ppermute(own, 'seq', OTHER_CORE)  1.86 us
  transfers between devices with their start and end apart: 2, of which 2 were waited for; matrix products, arithmetic and copies ran while one was open for 1% of the time, Pallas kernels for 0%

profile of v2, /device:TPU:1, one launch (start us, length us, event | category | flops | bytes accessed | tf_op | source)
XLA Modules:
  0.0 88.2 jit_solution(978391378978003285)
XLA Ops:
  0.0 6.0 %shard_map.55 = bf16[8,3,128,384]{3,2,1,0:T(8,128)(2,1)} custom-call(bf16[1,128,3072]{2,1,0:T(8,128)(2,1)} %q_ref.1, bf16[1,128,3072]{2,1,0:T(8,128)(2,1)} %k_ref.1, bf16[1,128,3072]{2,1,0:T(8,128)(2,1)} %v_ref.1), custom_call_target="tpu_custom_call" | custom-call | tf_op jit(solution)/shard_map/pallas_call | solution.py:151
  6.0 0.0 copy-start
  6.0 0.0 copy-start.1
  6.0 35.7 %all_to_all.10.q_ref.k_own.v_own = bf16[8,3,128,384]{3,2,1,0:T(8,128)(2,1)S(1)} all-to-all(bf16[8,3,128,384]{3,2,1,0:T(8,128)(2,1)} %shard_map.55), channel_id=1, replica_groups={{0,2,4,6,8,10,12,14},{1,3,5,7,9,11,13,15},{16,18,20,22,24,26,28,30},{17..., dimensions={0} | all-to-all | bytes 4718592 | tf_op jit(solution)/shard_map/all_to_all | solution.py:185
  41.7 1.9 %collective-permute-start = (bf16[8,3,128,384]{3,2,1,0:T(8,128)(2,1)S(1)}, bf16[8,3,128,384]{3,2,1,0:T(8,128)(2,1)}, u32[]{:S(2)}, u32[]{:S(2)}) collective-permute-start(bf16[8,3,128,384]{3,2,1,0:T(8,128)(2,1)S(1)} %all_to_all.10.q_ref.k_own.v_own), channel_id=1, source_target_pairs={{0,1},{1,0},{2,3},{3,2},{4,5},{5,4},{6,7},{7,6},{8,9},{9,8},{10,11... | collective-permute-start | bytes 7077896 | tf_op jit(solution)/shard_map/ppermute | solution.py:186
  43.5 0.0 copy-done
  43.5 0.1 pad_add_fusion
  43.6 0.0 collective-permute-start.1
  43.7 0.0 copy-done.1
  43.7 0.7 dynamic_slice.3.length_ref
  44.3 3.3 %collective-permute-done.1 = s32[3,16,128]{2,1,0:T(8,128)S(1)} collective-permute-done((s32[3,16,128]{2,1,0:T(8,128)S(1)}, s32[3,16,128]{2,1,0:T(8,128)S(1)}, u32[]{:S(2)}, u32[]{:S(2)}) %collective-permute-start.1) | collective-permute-done | bytes 24608 | tf_op jit(solution)/shard_map/ppermute | solution.py:181
  47.6 0.1 add_select_fusion.mask_ref
  47.7 0.2 collective-permute-done.k_sib.v_sib
  47.9 19.5 %shard_map.56 = bf16[8,128,384]{2,1,0:T(8,128)(2,1)S(1)} custom-call(s32[1]{0:T(128)} %bitcast.core_ref, s32[1]{0:T(128)} %dynamic_slice.3.length_ref, bf16[8,3,128,384]{3,2,1,0:T(8,128)(2,1)S(1)} %all_to_all.10.q_ref.k_own.v_own, bf16[8,3,128,384]{3,2,1,0:T(8,128)(2,1)S(1)} %all_to_all.10.q_ref.k_own.v_own, ...), custom_call_target="tpu_custom_call" | custom-call | flops 3221225472 | bytes 8388608 | tf_op jit(solution)/shard_map/pallas_call | solution.py:118
  67.4 15.7 %all_to_all.11.block_ref = bf16[8,128,384]{2,1,0:T(8,128)(2,1)} all-to-all(bf16[8,128,384]{2,1,0:T(8,128)(2,1)S(1)} %shard_map.56), channel_id=1, replica_groups={{0,2,4,6,8,10,12,14},{1,3,5,7,9,11,13,15},{16,18,20,22,24,26,28,30},{17..., dimensions={0} | all-to-all | bytes 1572864 | tf_op jit(solution)/shard_map/all_to_all | solution.py:188
  83.1 5.0 %shard_map.57 = bf16[1,128,3072]{2,1,0:T(8,128)(2,1)} custom-call(bf16[8,128,384]{2,1,0:T(8,128)(2,1)} %all_to_all.11.block_ref), custom_call_target="tpu_custom_call" | custom-call | tf_op jit(solution)/shard_map/pallas_call | solution.py:165
  (1 shorter events, 0.0 us)
Async XLA Ops:
  6.0 37.6 %copy-start = (s32[1,3,16,16]{3,2,1,0:T(8,128)S(1)}, s32[1,3,16,16]{3,2,1,0:T(8,128)}, u32[]{:S(2)}) copy-start(s32[1,3,16,16]{3,2,1,0:T(8,128)} %param.9) | copy-start | bytes 9220
  6.0 37.7 %copy-start.1 = (s32[16]{0:T(128)S(1)}, s32[16]{0:T(128)}, u32[]{:S(2)}) copy-start(s32[16]{0:T(128)} %param.8) | copy-start | bytes 196
  41.7 6.2 %collective-permute-start = (bf16[8,3,128,384]{3,2,1,0:T(8,128)(2,1)S(1)}, bf16[8,3,128,384]{3,2,1,0:T(8,128)(2,1)}, u32[]{:S(2)}, u32[]{:S(2)}) collective-permute-start(bf16[8,3,128,384]{3,2,1,0:T(8,128)(2,1)S(1)} %all_to_all.10.q_ref.k_own.v_own), channel_id=1, source_target_pairs={{0,1},{1,0},{2,3},{3,2},{4,5},{5,4},{6,7},{7,6},{8,9},{9,8},{10,11... | collective-permute-start | bytes 7077896 | tf_op jit(solution)/shard_map/ppermute | solution.py:186
  43.6 4.0 %collective-permute-start.1 = (s32[3,16,128]{2,1,0:T(8,128)S(1)}, s32[3,16,128]{2,1,0:T(8,128)S(1)}, u32[]{:S(2)}, u32[]{:S(2)}) collective-permute-start(s32[3,16,128]{2,1,0:T(8,128)S(1)} %pad_add_fusion), channel_id=1, source_target_pairs={{0,1},{1,0},{2,3},{3,2},{4,5},{5,4},{6,7},{7,6},{8,9},{9,8},{10,11... | collective-permute-start | bytes 73736 | tf_op jit(solution)/shard_map/ppermute | solution.py:181

commit v3 on v0

v3 whole, which is shorter than its diff:
```python
import functools

import jax
import jax.numpy as jnp
from jax import lax
from jax.experimental import pallas as pl
from jax.experimental.pallas import tpu as pltpu
from jax.sharding import PartitionSpec as P

TILE = 128
CHIPS = 8
PAIR = 128
PAIRS = 3
WIDTH = PAIRS * PAIR
QB = 2 * TILE
KB = 4 * TILE
CK = 256
MASKED = -1e30
SCALE = 0.125 * 1.4426950408889634

AWAY = ((0, 0), (1, 0), (1, 1), (3, 0), (3, 1), (2, 1), (0, 1), (2, 0))
WAVES = ((0, 1, 2), (3,))
OTHER_CORE = [(device, device ^ 1) for device in range(2 * CHIPS)]


def route(along_y, along_z):
    pairs = []
    for device in range(2 * CHIPS):
        y, z, core = device // 4, device // 2 % 2, device % 2
        pairs.append((device, (y + along_y) % 4 * 4 + (z ^ along_z) * 2 + core))
    return pairs


def matmul(a, b, dims):
    return lax.dot_general(a, b, (dims, ((), ())), preferred_element_type=jnp.float32)


def whereabouts():
    device = lax.axis_index("seq").astype(jnp.int32)
    y, z, core = device // 4, device // 2 % 2, device % 2
    to_chips = [(y + along_y) % 4 * 2 + (z + along_z) % 2 for along_y, along_z in AWAY]
    from_chips = [(y + 4 - along_y) % 4 * 2 + (z + along_z) % 2 for along_y, along_z in AWAY]
    return core, to_chips, from_chips


def wave_kernel(wave, lengths_ref, *refs):
    last = wave == len(WAVES) - 1
    new = WAVES[wave]
    seen = new[0]
    if wave == 0:
        mask_ref, other_mask_ref, *refs = refs
    else:
        bias_ref, *refs = refs
    blocks, others, refs = refs[: 2 * len(new)], refs[2 * len(new) : 3 * len(new)], refs[3 * len(new) :]
    old = [refs[i * 5 : i * 5 + 5] for i in range(seen)]
    refs = refs[5 * seen :]
    if last:
        out_ref, *refs = refs
    if wave == 0:
        bias_ref, *refs = refs
    made = [refs[3 * i : 3 * i + 3] for i in range(len(new))]
    refs = refs[3 * len(new) :]
    if not last:
        new_state = [refs[2 * u : 2 * u + 2] for u in range(seen + len(new))]
        refs = refs[2 * (seen + len(new)) :]
    scores = refs

    core, _, chips = whereabouts()
    length = lengths_ref[lax.axis_index("clip")]
    low = lax.broadcasted_iota(jnp.int32, (1, PAIR), 1) < 64
    column = lax.broadcasted_iota(jnp.int32, (TILE, PAIR), 1) & 63
    inside = lax.broadcasted_iota(jnp.int32, (TILE, PAIR), 0)

    if wave == 0:
        spread = (column[:16] == inside[:16]).astype(jnp.float32).astype(jnp.bfloat16)
        for number in range(2 * PAIRS):
            local = number % 3
            kept = jnp.where(core == number // 3, mask_ref[0, local], other_mask_ref[0, local])
            kept = matmul((kept - 1).astype(jnp.float32).astype(jnp.bfloat16), spread, ((1,), (0,)))
            bias_ref[number] = jnp.where(column[:16] == 16, MASKED, kept * -MASKED)

    for slot, block in enumerate(blocks):
        keys_new, values_new, queries_new = made[slot // 2]
        chip = chips[2 * seen + slot]
        for part in range(2):
            first = (2 * part + slot % 2) * TILE
            rows = slice(first, first + TILE)
            tile = 2 * chip + (core if part == 0 else 1 - core)
            dead = jnp.where(tile * TILE + inside >= length, 16, -1)
            hot = (column == tile) | (column == dead)
            hot = hot.astype(jnp.float32).astype(jnp.bfloat16)
            for pair in range(PAIRS):
                columns = slice(pair * PAIR, (pair + 1) * PAIR)
                if part == 0:
                    k, v = block[1, :, columns], block[2, :, columns]
                else:
                    other = others[slot // 2]
                    k, v = other[slot % 2, 0, :, columns], other[slot % 2, 1, :, columns]
                keys_new[2 * pair, rows, :] = jnp.where(low, k, hot)
                keys_new[2 * pair + 1, rows, :] = jnp.where(low, hot, k)
                values_new[columns, rows] = v.T
        first = slot % 2 * TILE
        for number in range(2 * PAIRS):
            bias = bias_ref[number, pl.ds(2 * chip + core, 1), :]
            bias = jnp.broadcast_to(bias, (TILE, PAIR)).astype(jnp.bfloat16)
            q = block[0, :, number // 2 * PAIR : (number // 2 + 1) * PAIR]
            q = jnp.where(low, q, bias) if number % 2 == 0 else jnp.where(low, bias, q)
            queries_new[number, first : first + TILE, :] = q

    keys = [group[0] for group in old + made]
    values = [group[1] for group in old + made]
    queries = [group[2] for group in old + made]

    every = tuple(range(seen + len(new)))
    items = []
    if seen:
        items += [(head, [(u, new) for u in range(seen)]) for head in range(2)]
    items += [(head, [(u, every)]) for u in new for head in range(2)]

    def chunks(item):
        return [(u, group, part) for u, groups in item[1] for group in groups for part in range(KB // CK)]

    def score_chunk(pair, index, place, tops):
        head = items[index][0]
        u, group, part = chunks(items[index])[place]
        number = 2 * pair + head
        s = matmul(keys[group][number, part * CK : (part + 1) * CK, :], queries[u][number], ((1,), (1,)))
        scores[index % 2][place * CK : (place + 1) * CK, :] = s
        top = jnp.max(s.reshape(CK // 8, 8, QB), axis=0)
        return {**tops, u: jnp.maximum(tops[u], top) if u in tops else top}

    def one_pair(pair, tops):
        finished = {}
        columns = pl.ds(pl.multiple_of(pair * PAIR, PAIR), PAIR)
        for index, item in enumerate(items):
            head = item[0]
            dims = pl.ds(pl.multiple_of(pair * PAIR + 64 * head, 64), 64)
            row_top, total, mixed = {}, {}, {}
            for u, _ in item[1]:
                row_top[u] = jnp.max(tops[u], axis=0, keepdims=True)
                total[u] = jnp.zeros((8, QB), jnp.float32)
                mixed[u] = jnp.zeros((64, QB), jnp.float32)
                if u < seen:
                    before = old[u][3][pair, head : head + 1, :]
                    row_top[u] = jnp.maximum(row_top[u], before)
                    fade = jnp.exp2((before - row_top[u]) * SCALE)
                    mixed[u] = old[u][4][dims, :] * fade
                    faded = old[u][3][pair, 8 + head : 9 + head, :] * fade
                    total[u] = jnp.where(lax.broadcasted_iota(jnp.int32, (8, QB), 0) == 0, faded, 0.0)
            now = chunks(item)
            following = (index + 1) % len(items)
            next_pair = pair if following else jnp.minimum(pair + 1, PAIRS - 1)
            later = len(chunks(items[following]))
            tops = {}
            done = 0
            for place, (u, group, part) in enumerate(now):
                until = (place + 1) * later // len(now)
                while done < until:
                    tops = score_chunk(next_pair, following, done, tops)
                    done += 1
                s = scores[index % 2][place * CK : (place + 1) * CK, :]
                weights = jnp.exp2((s - row_top[u]) * SCALE)
                total[u] = total[u] + jnp.sum(weights.reshape(CK // 8, 8, QB), axis=0)
                mixed[u] = mixed[u] + matmul(
                    values[group][dims, part * CK : (part + 1) * CK], weights.astype(jnp.bfloat16), ((1,), (0,))
                )
            for u, _ in item[1]:
                total[u] = jnp.sum(total[u], axis=0, keepdims=True)
                if not last:
                    new_state[u][0][pair, head : head + 1, :] = row_top[u]
                    new_state[u][0][pair, 8 + head : 9 + head, :] = total[u]
                    new_state[u][1][dims, :] = mixed[u]
                    continue
                finished[u, head] = mixed[u] / total[u]
                if head == 1:
                    query = lax.broadcasted_iota(jnp.int32, (1, QB), 1)
                    two = chips[2 * u : 2 * u + 2]
                    chip = jnp.where(query < TILE, two[0], two[1])
                    live = (2 * chip + core) * TILE + (query & (TILE - 1)) < length
                    both = jnp.concatenate([finished[u, 0], finished[u, 1]], axis=0)
                    both = jnp.where(live, both, 0.0).T.astype(jnp.bfloat16)
                    out_ref[two[0], :, columns] = both[:TILE]
                    out_ref[two[1], :, columns] = both[TILE:]
        return tops

    tops = {}
    for place in range(len(chunks(items[0]))):
        tops = score_chunk(0, 0, place, tops)
    lax.fori_loop(0, PAIRS, one_pair, tops)


def attend_wave(wave, lengths, masks, blocks, others, old):
    last = wave == len(WAVES) - 1
    new = WAVES[wave]
    bf16, f32 = jnp.bfloat16, jnp.float32
    kept = [((2 * PAIRS, KB, PAIR), bf16), ((WIDTH, KB), bf16), ((2 * PAIRS, QB, PAIR), bf16)] * len(new)
    groups = new[0] + len(new)
    made = [((2 * PAIRS, 16, PAIR), f32)] if wave == 0 else []
    made += kept + [((PAIRS, 16, QB), f32), ((WIDTH, QB), f32)] * groups
    operands = (lengths, *masks, *blocks, *others, *[array for group in old for array in group])
    scratch = [pltpu.VMEM((groups * KB, QB), f32)] * 2
    if last:
        out_shape = jax.ShapeDtypeStruct((CHIPS, TILE, WIDTH), bf16)
        scratch = [pltpu.VMEM(*array) for array in made[: len(made) - 2 * groups]] + scratch
        out_specs = pl.BlockSpec(memory_space=pltpu.VMEM)
    else:
        out_shape = [jax.ShapeDtypeStruct(*array) for array in made]
        out_specs = [pl.BlockSpec(memory_space=pltpu.VMEM)] * len(out_shape)
    out = pl.pallas_call(
        functools.partial(wave_kernel, wave),
        out_shape=out_shape,
        in_specs=[pl.BlockSpec(memory_space=pltpu.SMEM)]
        + [pl.BlockSpec(memory_space=pltpu.VMEM)] * (len(operands) - 1),
        out_specs=out_specs,
        scratch_shapes=scratch,
        compiler_params=pltpu.CompilerParams(vmem_limit_bytes=32 * 2**20),
        cost_estimate=pl.CostEstimate(flops=0, bytes_accessed=0, transcendentals=0),
    )(*operands)
    if last:
        return out
    if wave == 0:
        masks, out = out[:1], out[1:]
    kept, states = out[: 3 * len(new)], out[3 * len(new) :]
    parts = [group[:3] for group in old] + [kept[3 * i : 3 * i + 3] for i in range(len(new))]
    return masks, [(*part, *states[2 * u : 2 * u + 2]) for u, part in enumerate(parts)]


def split_kernel(q_ref, k_ref, v_ref, *refs):
    _, chips, _ = whereabouts()
    blocks, done = refs[:-1], refs[-1]
    copies = []
    for chip, block in zip(chips, blocks):
        columns = pl.ds(pl.multiple_of(chip * WIDTH, PAIR), WIDTH)
        for which, array in enumerate((q_ref, k_ref, v_ref)):
            copies.append(pltpu.make_async_copy(array.at[0, :, columns], block.at[which], done.at[len(copies)]))
    for copy in copies:
        copy.start()
    for copy in copies:
        copy.wait()


def split_columns(*arrays):
    return pl.pallas_call(
        split_kernel,
        out_shape=[jax.ShapeDtypeStruct((3, TILE, WIDTH), jnp.bfloat16)] * CHIPS,
        in_specs=[pl.BlockSpec(memory_space=pl.ANY)] * 3,
        out_specs=[pl.BlockSpec(memory_space=pltpu.VMEM)] * CHIPS,
        scratch_shapes=[pltpu.SemaphoreType.DMA((3 * CHIPS,))],
    )(*arrays)


def join_kernel(blocks_ref, rows_ref, done):
    copies = [
        pltpu.make_async_copy(
            blocks_ref.at[chip], rows_ref.at[0, :, pl.ds(chip * WIDTH, WIDTH)], done.at[chip]
        )
        for chip in range(CHIPS)
    ]
    for copy in copies:
        copy.start()
    for copy in copies:
        copy.wait()


def join_columns(blocks):
    return pl.pallas_call(
        join_kernel,
        out_shape=jax.ShapeDtypeStruct((1, TILE, CHIPS * WIDTH), jnp.bfloat16),
        in_specs=[pl.BlockSpec(memory_space=pltpu.VMEM)],
        out_specs=pl.BlockSpec(memory_space=pl.ANY),
        scratch_shapes=[pltpu.SemaphoreType.DMA((CHIPS,))],
    )(blocks)


def after(array, earlier):
    return lax.optimization_barrier((array, earlier))[0]


def on_device(queries, key_states, value_states, clip_lengths, tile_masks):
    masks = tile_masks, lax.ppermute(tile_masks, "seq", OTHER_CORE)
    sent = list(split_columns(queries, key_states, value_states))
    sent[3] = after(sent[3], masks[1])
    blocks = [sent[0]]
    for slot in range(1, CHIPS):
        blocks.append(lax.ppermute(sent[slot], "seq", route(*AWAY[slot])))

    groups = []
    for wave, new in enumerate(WAVES):
        now = blocks[2 * new[0] : 2 * new[-1] + 2]
        if wave > 0:
            now = after(now, groups[0][3])
        others = [
            lax.ppermute(jnp.stack([block[1:] for block in now[i : i + 2]]), "seq", OTHER_CORE)
            for i in range(0, len(now), 2)
        ]
        out = attend_wave(wave, clip_lengths, masks, now, others, groups)
        if wave < len(WAVES) - 1:
            masks, groups = out

    every = [[2 * chip + core for chip in range(CHIPS)] for core in range(2)]
    back = lax.all_to_all(out, "seq", 0, 0, tiled=True, axis_index_groups=every)
    return join_columns(back)


def solution(mesh):
    split = P("clip", "seq", None)
    return jax.shard_map(
        on_device,
        mesh=mesh,
        in_specs=(split, split, split, P(), P("clip", "seq", None, None)),
        out_specs=split,
        check_vma=False,
    )
```

time: 169 us -> 75.9 us (0.45)
  the two profiles are of different devices: /device:TPU:163 before, /device:TPU:1 now
where the time goes in v3:
time: 75.9 us; the launch traced here: 75.3 us
  Pallas kernels  24.8 us (33%)
  waiting for transfers between devices  17 us (22%)
  blocking collectives  16.1 us (21%)
  starting transfers between devices  15 us (20%)
  local copies, waits for them, and re-layouts  1.94 us (3%)
    pallas_call x2, Pallas kernels, attend_wave(): pl.pallas_call(functools.partial(wave_kernel, wave), out_shape=out_shape,...  19.4 us
    all_to_all x1, blocking collectives, on_device(): back = lax.all_to_all(out, 'seq', 0, 0, tiled=True, axis_index_groups=every)  16.1 us
    ppermute x7, waiting for transfers between devices, on_device(): blocks.append(lax.ppermute(sent[slot], 'seq', route(*AWAY[slot])))  15.5 us
    ppermute x7, starting transfers between devices, on_device(): blocks.append(lax.ppermute(sent[slot], 'seq', route(*AWAY[slot])))  10.5 us
    ppermute x4, starting transfers between devices, on_device(): lax.ppermute(jnp.stack([block[1:] for block in now[i:i + 2]]), 'seq', OTH...  3.49 us
    pallas_call x1, Pallas kernels, split_columns(): pl.pallas_call(split_kernel, out_shape=[jax.ShapeDtypeStruct((3, TILE, WI...  3.35 us
    pallas_call x1, Pallas kernels, join_columns(): pl.pallas_call(join_kernel, out_shape=jax.ShapeDtypeStruct((1, TILE, CHIP...  2.07 us
    ppermute x4, waiting for transfers between devices, on_device(): lax.ppermute(jnp.stack([block[1:] for block in now[i:i + 2]]), 'seq', OTH...  1.52 us
  transfers between devices with their start and end apart: 12, of which 4 were waited for; matrix products, arithmetic and copies ran while one was open for 2% of the time, Pallas kernels for 15%

profile of v3, /device:TPU:1, one launch (start us, length us, event | category | flops | bytes accessed | tf_op | source)
XLA Modules:
  0.0 75.3 jit_solution(13598296501085336911)
XLA Ops:
  0.0 3.4 %shard_map.55 = (bf16[3,128,384]{2,1,0:T(8,128)(2,1)}, bf16[3,128,384]{2,1,0:T(8,128)(2,1)}, bf16[3,128,384]{2,1,0:T(8,128)(2,1)}, bf16[3,128,384]{2,1,0:T(8,128...) custom-call(bf16[1,128,3072]{2,1,0:T(8,128)(2,1)} %q_ref.1, ...), custom_call_target="tpu_custom_call" | custom-call | tf_op jit(solution)/shard_map/pallas_call | solution.py:243
  3.4 5.0 %collective-permute-start.4 = (bf16[3,128,384]{2,1,0:T(8,128)(2,1)}, bf16[3,128,384]{2,1,0:T(8,128)(2,1)S(1)}, u32[]{:S(2)}, u32[]{:S(2)}) collective-permute-start(bf16[3,128,384]{2,1,0:T(8,128)(2,1)} %get-tuple-element.37), channel_id=1, source_target_pairs={{0,14},{1,15},{2,12},{3,13},{4,2},{5,3},{6,0},{7,1},{8,6},{9,7},{1... | collective-permute-start | bytes 884744 | tf_op jit(solution)/shard_map/ppermute | solution.py:285
  8.4 1.0 %collective-permute-start = (s32[1,3,16,16]{3,2,1,0:T(8,128)S(1)}, s32[1,3,16,16]{3,2,1,0:T(8,128)S(1)}, u32[]{:S(2)}, u32[]{:S(2)}) collective-permute-start(s32[1,3,16,16]{3,2,1,0:T(8,128)S(1)} %copy-done.1), channel_id=1, source_target_pairs={{0,1},{1,0},{2,3},{3,2},{4,5},{5,4},{6,7},{7,6},{8,9},{9,8},{10,11... | collective-permute-start | bytes 9224 | tf_op jit(solution)/shard_map/ppermute | solution.py:280
  9.3 0.0 collective-permute-start.1
  9.3 0.0 collective-permute-start.2
  9.4 4.7 %collective-permute-start.5 = (bf16[3,128,384]{2,1,0:T(8,128)(2,1)}, bf16[3,128,384]{2,1,0:T(8,128)(2,1)S(1)}, u32[]{:S(2)}, u32[]{:S(2)}) collective-permute-start(bf16[3,128,384]{2,1,0:T(8,128)(2,1)} %get-tuple-element.38), channel_id=1, source_target_pairs={{0,10},{1,11},{2,8},{3,9},{4,14},{5,15},{6,12},{7,13},{8,2},{9,3},... | collective-permute-start | bytes 884744 | tf_op jit(solution)/shard_map/ppermute | solution.py:285
  14.1 0.9 %slice_bitcast_fusion.7 = bf16[1,2,128,384]{3,2,1,0:T(8,128)(2,1)S(1)} fusion(bf16[3,128,384]{2,1,0:T(8,128)(2,1)} %get-tuple-element.32.refs_2_), kind=kLoop, calls=%fused_computation.11 | loop fusion | bytes 393216 | tf_op jit(solution)/shard_map/stack | solution.py:293
  15.1 0.1 collective-permute-start.3
  15.2 13.2 %collective-permute-done.5.refs_7_ = bf16[3,128,384]{2,1,0:T(8,128)(2,1)S(1)} collective-permute-done((bf16[3,128,384]{2,1,0:T(8,128)(2,1)}, bf16[3,128,384]{2,1,0:T(8,128)(2,1)S(1)}, u32[]{:S(2)}, u32[]{:S(2)}) %collective-permute-start.5) | collective-permute-done | bytes 294944 | tf_op jit(solution)/shard_map/ppermute | solution.py:285
  28.5 1.3 %collective-permute-start.8 = (bf16[2,2,128,384]{3,2,1,0:T(8,128)(2,1)S(1)}, bf16[2,2,128,384]{3,2,1,0:T(8,128)(2,1)S(1)}, u32[]{:S(2)}, u32[]{:S(2)}) collective-permute-start(bf16[2,2,128,384]{3,2,1,0:T(8,128)(2,1)S(1)} %pad_maximum_fusion.2), channel_id=1, source_target_pairs={{0,1},{1,0},{2,3},{3,2},{4,5},{5,4},{6,7},{7,6},{8,9},{9,8},{10,11... | collective-permute-start | bytes 1179656 | tf_op jit(solution)/shard_map/ppermute | solution.py:293
  29.8 2.2 %collective-permute-done.1.refs_3_ = bf16[3,128,384]{2,1,0:T(8,128)(2,1)S(1)} collective-permute-done((bf16[3,128,384]{2,1,0:T(8,128)(2,1)}, bf16[3,128,384]{2,1,0:T(8,128)(2,1)S(1)}, u32[]{:S(2)}, u32[]{:S(2)}) %collective-permute-start.1) | collective-permute-done | bytes 294944 | tf_op jit(solution)/shard_map/ppermute | solution.py:285
  32.1 0.9 %collective-permute-start.6 = (bf16[2,2,128,384]{3,2,1,0:T(8,128)(2,1)S(1)}, bf16[2,2,128,384]{3,2,1,0:T(8,128)(2,1)S(1)}, u32[]{:S(2)}, u32[]{:S(2)}) collective-permute-start(bf16[2,2,128,384]{3,2,1,0:T(8,128)(2,1)S(1)} %pad_maximum_fusion), channel_id=1, source_target_pairs={{0,1},{1,0},{2,3},{3,2},{4,5},{5,4},{6,7},{7,6},{8,9},{9,8},{10,11... | collective-permute-start | bytes 1179656 | tf_op jit(solution)/shard_map/ppermute | solution.py:293
  33.1 0.0 copy-start
  33.1 0.1 collective-permute-start.7
  33.2 0.7 copy-done.4
  34.0 0.1 copy-done.3
  34.1 0.7 collective-permute-start.10
  34.8 0.2 collective-permute-done.7.refs_9_
  34.9 11.4 %shard_map.56 = (f32[6,16,128]{2,1,0:T(8,128)S(1)}, bf16[6,512,128]{2,1,0:T(8,128)(2,1)S(1)}, bf16[384,512]{1,0:T(8,128)(2,1)S(1)}, bf16[6,256,128]{2,1,0:T(8,12...) custom-call(s32[16]{0:T(128)S(1)} %copy-done.2, ...), custom_call_target="tpu_custom_call" | custom-call | tf_op jit(solution)/shard_map/pallas_call | solution.py:209
  46.4 1.2 %collective-permute-start.11 = (bf16[2,2,128,384]{3,2,1,0:T(8,128)(2,1)S(1)}, bf16[2,2,128,384]{3,2,1,0:T(8,128)(2,1)S(1)}, u32[]{:S(2)}, u32[]{:S(2)}) collective-permute-start(bf16[2,2,128,384]{3,2,1,0:T(8,128)(2,1)S(1)} %pad_maximum_fusion.3), channel_id=1, source_target_pairs={{0,1},{1,0},{2,3},{3,2},{4,5},{5,4},{6,7},{7,6},{8,9},{9,8},{10,11... | collective-permute-start | bytes 1179656 | tf_op jit(solution)/shard_map/ppermute | solution.py:293
  47.6 1.3 %collective-permute-done.11.refs_3_ = bf16[2,2,128,384]{3,2,1,0:T(8,128)(2,1)S(1)} collective-permute-done((bf16[2,2,128,384]{3,2,1,0:T(8,128)(2,1)S(1)}, bf16[2,2,128,384]{3,2,1,0:T(8,128)(2,1)S(1)}, u32[]{:S(2)}, u32[]{:S(2)}) %collective-permute-start.11) | collective-permute-done | bytes 393248 | tf_op jit(solution)/shard_map/ppermute | solution.py:293
  49.0 8.0 %shard_map.57 = bf16[8,128,384]{2,1,0:T(8,128)(2,1)S(1)} custom-call(s32[16]{0:T(128)S(1)} %copy-done.2, f32[6,16,128]{2,1,0:T(8,128)S(1)} %get-tuple-element.39.refs_0_, bf16[3,128,384]{2,1,0:T(8,128)(2,1)S(1)} %collective-permute-done.9.refs_1_, bf16[3,128,384]{2,1,0:T(8,128)(2,1)S(1)} %collective-permute-done.10.refs_2_, ...), custom_call_target="tpu_custom_call" | custom-call | tf_op jit(solution)/shard_map/pallas_call | solution.py:209
  57.0 16.1 %all_to_all.5.blocks_ref = bf16[8,128,384]{2,1,0:T(8,128)(2,1)} all-to-all(bf16[8,128,384]{2,1,0:T(8,128)(2,1)S(1)} %shard_map.57), channel_id=1, replica_groups={{0,2,4,6,8,10,12,14},{1,3,5,7,9,11,13,15},{16,18,20,22,24,26,28,30},{17..., dimensions={0} | all-to-all | bytes 1572864 | tf_op jit(solution)/shard_map/all_to_all | solution.py:301
  73.1 2.1 %shard_map.58 = bf16[1,128,3072]{2,1,0:T(8,128)(2,1)} custom-call(bf16[8,128,384]{2,1,0:T(8,128)(2,1)} %all_to_all.5.blocks_ref), custom_call_target="tpu_custom_call" | custom-call | tf_op jit(solution)/shard_map/pallas_call | solution.py:266
  (28 shorter events, 0.4 us)
Async XLA Ops:
  0.0 8.4 %copy-start.1 = (s32[1,3,16,16]{3,2,1,0:T(8,128)S(1)}, s32[1,3,16,16]{3,2,1,0:T(8,128)}, u32[]{:S(2)}) copy-start(s32[1,3,16,16]{3,2,1,0:T(8,128)} %refs_0_.1) | copy-start | bytes 9220
  3.4 11.7 %copy-start.5 = (bf16[3,128,384]{2,1,0:T(8,128)(2,1)S(1)}, bf16[3,128,384]{2,1,0:T(8,128)(2,1)}, u32[]{:S(2)}) copy-start(bf16[3,128,384]{2,1,0:T(8,128)(2,1)} %get-tuple-element.36) | copy-start | bytes 884740
  3.4 11.8 %collective-permute-start.4 = (bf16[3,128,384]{2,1,0:T(8,128)(2,1)}, bf16[3,128,384]{2,1,0:T(8,128)(2,1)S(1)}, u32[]{:S(2)}, u32[]{:S(2)}) collective-permute-start(bf16[3,128,384]{2,1,0:T(8,128)(2,1)} %get-tuple-element.37), channel_id=1, source_target_pairs={{0,14},{1,15},{2,12},{3,13},{4,2},{5,3},{6,0},{7,1},{8,6},{9,7},{1... | collective-permute-start | bytes 884744 | tf_op jit(solution)/shard_map/ppermute | solution.py:285
  8.4 6.7 %collective-permute-start = (s32[1,3,16,16]{3,2,1,0:T(8,128)S(1)}, s32[1,3,16,16]{3,2,1,0:T(8,128)S(1)}, u32[]{:S(2)}, u32[]{:S(2)}) collective-permute-start(s32[1,3,16,16]{3,2,1,0:T(8,128)S(1)} %copy-done.1), channel_id=1, source_target_pairs={{0,1},{1,0},{2,3},{3,2},{4,5},{5,4},{6,7},{7,6},{8,9},{9,8},{10,11... | collective-permute-start | bytes 9224 | tf_op jit(solution)/shard_map/ppermute | solution.py:280
  9.3 22.7 %collective-permute-start.1 = (bf16[3,128,384]{2,1,0:T(8,128)(2,1)}, bf16[3,128,384]{2,1,0:T(8,128)(2,1)S(1)}, u32[]{:S(2)}, u32[]{:S(2)}) collective-permute-start(bf16[3,128,384]{2,1,0:T(8,128)(2,1)} %get-tuple-element.33), channel_id=1, source_target_pairs={{0,4},{1,5},{2,6},{3,7},{4,8},{5,9},{6,10},{7,11},{8,12},{9,13},{1... | collective-permute-start | bytes 884744 | tf_op jit(solution)/shard_map/ppermute | solution.py:285
  9.3 23.7 %collective-permute-start.2 = (bf16[3,128,384]{2,1,0:T(8,128)(2,1)}, bf16[3,128,384]{2,1,0:T(8,128)(2,1)S(1)}, u32[]{:S(2)}, u32[]{:S(2)}) collective-permute-start(bf16[3,128,384]{2,1,0:T(8,128)(2,1)} %get-tuple-element.34), channel_id=1, source_target_pairs={{0,6},{1,7},{2,4},{3,5},{4,10},{5,11},{6,8},{7,9},{8,14},{9,15},{1... | collective-permute-start | bytes 884744 | tf_op jit(solution)/shard_map/ppermute | solution.py:285
  9.4 19.0 %collective-permute-start.5 = (bf16[3,128,384]{2,1,0:T(8,128)(2,1)}, bf16[3,128,384]{2,1,0:T(8,128)(2,1)S(1)}, u32[]{:S(2)}, u32[]{:S(2)}) collective-permute-start(bf16[3,128,384]{2,1,0:T(8,128)(2,1)} %get-tuple-element.38), channel_id=1, source_target_pairs={{0,10},{1,11},{2,8},{3,9},{4,14},{5,15},{6,12},{7,13},{8,2},{9,3},... | collective-permute-start | bytes 884744 | tf_op jit(solution)/shard_map/ppermute | solution.py:285
  15.1 18.0 %collective-permute-start.3 = (bf16[3,128,384]{2,1,0:T(8,128)(2,1)S(1)}, bf16[3,128,384]{2,1,0:T(8,128)(2,1)S(1)}, u32[]{:S(2)}, u32[]{:S(2)}) collective-permute-start(bf16[3,128,384]{2,1,0:T(8,128)(2,1)S(1)} %copy-done.5), channel_id=1, source_target_pairs={{0,12},{1,13},{2,14},{3,15},{4,0},{5,1},{6,2},{7,3},{8,4},{9,5},{1... | collective-permute-start | bytes 884744 | tf_op jit(solution)/shard_map/ppermute | solution.py:285
  28.5 6.3 %collective-permute-start.8 = (bf16[2,2,128,384]{3,2,1,0:T(8,128)(2,1)S(1)}, bf16[2,2,128,384]{3,2,1,0:T(8,128)(2,1)S(1)}, u32[]{:S(2)}, u32[]{:S(2)}) collective-permute-start(bf16[2,2,128,384]{3,2,1,0:T(8,128)(2,1)S(1)} %pad_maximum_fusion.2), channel_id=1, source_target_pairs={{0,1},{1,0},{2,3},{3,2},{4,5},{5,4},{6,7},{7,6},{8,9},{9,8},{10,11... | collective-permute-start | bytes 1179656 | tf_op jit(solution)/shard_map/ppermute | solution.py:293
  32.1 2.7 %collective-permute-start.6 = (bf16[2,2,128,384]{3,2,1,0:T(8,128)(2,1)S(1)}, bf16[2,2,128,384]{3,2,1,0:T(8,128)(2,1)S(1)}, u32[]{:S(2)}, u32[]{:S(2)}) collective-permute-start(bf16[2,2,128,384]{3,2,1,0:T(8,128)(2,1)S(1)} %pad_maximum_fusion), channel_id=1, source_target_pairs={{0,1},{1,0},{2,3},{3,2},{4,5},{5,4},{6,7},{7,6},{8,9},{9,8},{10,11... | collective-permute-start | bytes 1179656 | tf_op jit(solution)/shard_map/ppermute | solution.py:293
  33.0 1.0 %copy-start.4 = (bf16[3,128,384]{2,1,0:T(8,128)(2,1)S(1)}, bf16[3,128,384]{2,1,0:T(8,128)(2,1)}, u32[]{:S(2)}) copy-start(bf16[3,128,384]{2,1,0:T(8,128)(2,1)} %get-tuple-element.40) | copy-start | bytes 884740
  33.1 1.0 %copy-start.3 = (bf16[3,128,384]{2,1,0:T(8,128)(2,1)S(1)}, bf16[3,128,384]{2,1,0:T(8,128)(2,1)}, u32[]{:S(2)}) copy-start(bf16[3,128,384]{2,1,0:T(8,128)(2,1)} %get-tuple-element.41) | copy-start | bytes 884740
  33.1 1.9 %copy-start = (bf16[3,128,384]{2,1,0:T(8,128)(2,1)S(1)}, bf16[3,128,384]{2,1,0:T(8,128)(2,1)}, u32[]{:S(2)}) copy-start(bf16[3,128,384]{2,1,0:T(8,128)(2,1)} %get-tuple-element.32.refs_2_) | copy-start | bytes 884740
  33.1 1.8 %collective-permute-start.7 = (bf16[2,2,128,384]{3,2,1,0:T(8,128)(2,1)S(1)}, bf16[2,2,128,384]{3,2,1,0:T(8,128)(2,1)S(1)}, u32[]{:S(2)}, u32[]{:S(2)}) collective-permute-start(bf16[2,2,128,384]{3,2,1,0:T(8,128)(2,1)S(1)} %pad_maximum_fusion.1), channel_id=1, source_target_pairs={{0,1},{1,0},{2,3},{3,2},{4,5},{5,4},{6,7},{7,6},{8,9},{9,8},{10,11... | collective-permute-start | bytes 1179656 | tf_op jit(solution)/shard_map/ppermute | solution.py:293
  34.0 1.0 %copy-start.2 = (s32[16]{0:T(128)S(1)}, s32[16]{0:T(128)}, u32[]{:S(2)}) copy-start(s32[16]{0:T(128)} %lengths_ref.3) | copy-start | bytes 196
  34.0 12.3 %collective-permute-start.9 = (bf16[3,128,384]{2,1,0:T(8,128)(2,1)S(1)}, bf16[3,128,384]{2,1,0:T(8,128)(2,1)S(1)}, u32[]{:S(2)}, u32[]{:S(2)}) collective-permute-start(bf16[3,128,384]{2,1,0:T(8,128)(2,1)S(1)} %copy-done.4), channel_id=1, source_target_pairs={{0,2},{1,3},{2,0},{3,1},{4,6},{5,7},{6,4},{7,5},{8,10},{9,11},{10,... | collective-permute-start | bytes 884744 | tf_op jit(solution)/shard_map/ppermute | solution.py:285
  34.1 12.3 %collective-permute-start.10 = (bf16[3,128,384]{2,1,0:T(8,128)(2,1)S(1)}, bf16[3,128,384]{2,1,0:T(8,128)(2,1)S(1)}, u32[]{:S(2)}, u32[]{:S(2)}) collective-permute-start(bf16[3,128,384]{2,1,0:T(8,128)(2,1)S(1)} %copy-done.3), channel_id=1, source_target_pairs={{0,8},{1,9},{2,10},{3,11},{4,12},{5,13},{6,14},{7,15},{8,0},{9,1},... | collective-permute-start | bytes 884744 | tf_op jit(solution)/shard_map/ppermute | solution.py:285
  46.4 2.5 %collective-permute-start.11 = (bf16[2,2,128,384]{3,2,1,0:T(8,128)(2,1)S(1)}, bf16[2,2,128,384]{3,2,1,0:T(8,128)(2,1)S(1)}, u32[]{:S(2)}, u32[]{:S(2)}) collective-permute-start(bf16[2,2,128,384]{3,2,1,0:T(8,128)(2,1)S(1)} %pad_maximum_fusion.3), channel_id=1, source_target_pairs={{0,1},{1,0},{2,3},{3,2},{4,5},{5,4},{6,7},{7,6},{8,9},{9,8},{10,11... | collective-permute-start | bytes 1179656 | tf_op jit(solution)/shard_map/ppermute | solution.py:293

commit v4 on v3

--- a/solution.py
+++ b/solution.py
@@ -20,6 +20,7 @@
 
 AWAY = ((0, 0), (1, 0), (1, 1), (3, 0), (3, 1), (2, 1), (0, 1), (2, 0))
 WAVES = ((0, 1, 2), (3,))
+SPLITS = ((5,), (1, 2, 3, 4), (0, 6, 7))
 OTHER_CORE = [(device, device ^ 1) for device in range(2 * CHIPS)]
 
 
@@ -225,12 +226,12 @@
     return masks, [(*part, *states[2 * u : 2 * u + 2]) for u, part in enumerate(parts)]
 
 
-def split_kernel(q_ref, k_ref, v_ref, *refs):
+def split_kernel(slots, q_ref, k_ref, v_ref, *refs):
     _, chips, _ = whereabouts()
     blocks, done = refs[:-1], refs[-1]
     copies = []
-    for chip, block in zip(chips, blocks):
-        columns = pl.ds(pl.multiple_of(chip * WIDTH, PAIR), WIDTH)
+    for slot, block in zip(slots, blocks):
+        columns = pl.ds(pl.multiple_of(chips[slot] * WIDTH, PAIR), WIDTH)
         for which, array in enumerate((q_ref, k_ref, v_ref)):
             copies.append(pltpu.make_async_copy(array.at[0, :, columns], block.at[which], done.at[len(copies)]))
     for copy in copies:
@@ -239,13 +240,13 @@
         copy.wait()
 
 
-def split_columns(*arrays):
+def split_columns(slots, *arrays):
     return pl.pallas_call(
-        split_kernel,
-        out_shape=[jax.ShapeDtypeStruct((3, TILE, WIDTH), jnp.bfloat16)] * CHIPS,
+        functools.partial(split_kernel, slots),
+        out_shape=[jax.ShapeDtypeStruct((3, TILE, WIDTH), jnp.bfloat16)] * len(slots),
         in_specs=[pl.BlockSpec(memory_space=pl.ANY)] * 3,
-        out_specs=[pl.BlockSpec(memory_space=pltpu.VMEM)] * CHIPS,
-        scratch_shapes=[pltpu.SemaphoreType.DMA((3 * CHIPS,))],
+        out_specs=[pl.BlockSpec(memory_space=pltpu.VMEM)] * len(slots),
+        scratch_shapes=[pltpu.SemaphoreType.DMA((3 * len(slots),))],
     )(*arrays)
 
 
@@ -278,8 +279,10 @@
 
 def on_device(queries, key_states, value_states, clip_lengths, tile_masks):
     masks = tile_masks, lax.ppermute(tile_masks, "seq", OTHER_CORE)
-    sent = list(split_columns(queries, key_states, value_states))
-    sent[3] = after(sent[3], masks[1])
+    sent = [None] * CHIPS
+    for slots in SPLITS:
+        for slot, block in zip(slots, split_columns(slots, queries, key_states, value_states)):
+            sent[slot] = block
     blocks = [sent[0]]
     for slot in range(1, CHIPS):
         blocks.append(lax.ppermute(sent[slot], "seq", route(*AWAY[slot])))

time: 75.9 us -> 73.5 us (0.968)
  waiting for transfers between devices: 17 us -> 10.7 us
  Pallas kernels: 24.8 us -> 28 us
  starting transfers between devices: 15 us -> 16.4 us
    ppermute x7, waiting for transfers between devices: 15.5 us -> 9.3 us  [on_device(): blocks.append(lax.ppermute(sent[slot], 'seq', route(*AWAY[slot])))]
    pallas_call x1 -> x3, Pallas kernels: 3.35 us -> 6.51 us  [split_columns(): pl.pallas_call(functools.partial(split_kernel, slots), out_shape=[jax.Sha...]
    ppermute x7, starting transfers between devices: 10.5 us -> 12.7 us  [on_device(): blocks.append(lax.ppermute(sent[slot], 'seq', route(*AWAY[slot])))]
  transfers between devices with their start and end apart: 12 -> 12, of which waited for: 4 -> 2; matrix products, arithmetic and copies ran while one was open for 2% -> 2% of each run, Pallas kernels for 15% -> 22%
where the time goes in v4:
time: 73.5 us; the launch traced here: 72.9 us
  Pallas kernels  28 us (38%)
  starting transfers between devices  16.4 us (22%)
  blocking collectives  16 us (22%)
  waiting for transfers between devices  10.7 us (15%)
  local copies, waits for them, and re-layouts  1.25 us (2%)
    pallas_call x2, Pallas kernels, attend_wave(): pl.pallas_call(functools.partial(wave_kernel, wave), out_shape=out_shape,...  19.4 us
    all_to_all x1, blocking collectives, on_device(): back = lax.all_to_all(out, 'seq', 0, 0, tiled=True, axis_index_groups=every)  16 us
    ppermute x7, starting transfers between devices, on_device(): blocks.append(lax.ppermute(sent[slot], 'seq', route(*AWAY[slot])))  12.7 us
    ppermute x7, waiting for transfers between devices, on_device(): blocks.append(lax.ppermute(sent[slot], 'seq', route(*AWAY[slot])))  9.3 us
    pallas_call x3, Pallas kernels, split_columns(): pl.pallas_call(functools.partial(split_kernel, slots), out_shape=[jax.Sha...  6.51 us
    ppermute x4, starting transfers between devices, on_device(): lax.ppermute(jnp.stack([block[1:] for block in now[i:i + 2]]), 'seq', OTH...  3.22 us
    pallas_call x1, Pallas kernels, join_columns(): pl.pallas_call(join_kernel, out_shape=jax.ShapeDtypeStruct((1, TILE, CHIP...  2.07 us
  transfers between devices with their start and end apart: 12, of which 2 were waited for; matrix products, arithmetic and copies ran while one was open for 2% of the time, Pallas kernels for 22%

profile of v4, /device:TPU:1, one launch (start us, length us, event | category | flops | bytes accessed | tf_op | source)
XLA Modules:
  0.0 72.9 jit_solution(1945966516562644517)
XLA Ops:
  0.0 1.8 %shard_map.57 = bf16[3,128,384]{2,1,0:T(8,128)(2,1)} custom-call(bf16[1,128,3072]{2,1,0:T(8,128)(2,1)} %q_ref.5, bf16[1,128,3072]{2,1,0:T(8,128)(2,1)} %k_ref.5, bf16[1,128,3072]{2,1,0:T(8,128)(2,1)} %v_ref.5), custom_call_target="tpu_custom_call" | custom-call | tf_op jit(solution)/shard_map/pallas_call | solution.py:244
  1.8 5.2 %collective-permute-start.5 = (bf16[3,128,384]{2,1,0:T(8,128)(2,1)}, bf16[3,128,384]{2,1,0:T(8,128)(2,1)S(1)}, u32[]{:S(2)}, u32[]{:S(2)}) collective-permute-start(bf16[3,128,384]{2,1,0:T(8,128)(2,1)} %shard_map.57), channel_id=1, source_target_pairs={{0,10},{1,11},{2,8},{3,9},{4,14},{5,15},{6,12},{7,13},{8,2},{9,3},... | collective-permute-start | bytes 884744 | tf_op jit(solution)/shard_map/ppermute | solution.py:288
  6.9 2.5 %shard_map.56 = (bf16[3,128,384]{2,1,0:T(8,128)(2,1)}, bf16[3,128,384]{2,1,0:T(8,128)(2,1)}, bf16[3,128,384]{2,1,0:T(8,128)(2,1)}, bf16[3,128,384]{2,1,0:T(8,128)(2,1)}) custom-call(bf16[1,128,3072]{2,1,0:T(8,128)(2,1)} %q_ref.5, bf16[1,128,3072]{2,1,0:T(8,128)(2,1)} %k_ref.5, bf16[1,128,3072]{2,1,0:T(8,128)(2,1)} %v_ref.5), custom_call_target="tpu_custom_call" | custom-call | tf_op jit(solution)/shard_map/pallas_call | solution.py:244
  9.5 0.5 collective-permute-start.1
  10.0 2.3 %collective-permute-start.3 = (bf16[3,128,384]{2,1,0:T(8,128)(2,1)}, bf16[3,128,384]{2,1,0:T(8,128)(2,1)S(1)}, u32[]{:S(2)}, u32[]{:S(2)}) collective-permute-start(bf16[3,128,384]{2,1,0:T(8,128)(2,1)} %get-tuple-element.33), channel_id=1, source_target_pairs={{0,12},{1,13},{2,14},{3,15},{4,0},{5,1},{6,2},{7,3},{8,4},{9,5},{1... | collective-permute-start | bytes 884744 | tf_op jit(solution)/shard_map/ppermute | solution.py:288
  12.2 2.4 %collective-permute-start.4 = (bf16[3,128,384]{2,1,0:T(8,128)(2,1)}, bf16[3,128,384]{2,1,0:T(8,128)(2,1)S(1)}, u32[]{:S(2)}, u32[]{:S(2)}) collective-permute-start(bf16[3,128,384]{2,1,0:T(8,128)(2,1)} %get-tuple-element.34), channel_id=1, source_target_pairs={{0,14},{1,15},{2,12},{3,13},{4,2},{5,3},{6,0},{7,1},{8,6},{9,7},{1... | collective-permute-start | bytes 884744 | tf_op jit(solution)/shard_map/ppermute | solution.py:288
  14.6 2.2 %shard_map.55 = (bf16[3,128,384]{2,1,0:T(8,128)(2,1)}, bf16[3,128,384]{2,1,0:T(8,128)(2,1)}, bf16[3,128,384]{2,1,0:T(8,128)(2,1)}) custom-call(bf16[1,128,3072]{2,1,0:T(8,128)(2,1)} %q_ref.5, bf16[1,128,3072]{2,1,0:T(8,128)(2,1)} %k_ref.5, bf16[1,128,3072]{2,1,0:T(8,128)(2,1)} %v_ref.5), custom_call_target="tpu_custom_call" | custom-call | tf_op jit(solution)/shard_map/pallas_call | solution.py:244
  16.8 1.0 %slice_bitcast_fusion.7 = bf16[1,2,128,384]{3,2,1,0:T(8,128)(2,1)S(1)} fusion(bf16[3,128,384]{2,1,0:T(8,128)(2,1)} %get-tuple-element.30.refs_2_), kind=kLoop, calls=%fused_computation.11 | loop fusion | bytes 393216 | tf_op jit(solution)/shard_map/stack | solution.py:296
  17.8 9.3 %collective-permute-done.4.refs_6_ = bf16[3,128,384]{2,1,0:T(8,128)(2,1)S(1)} collective-permute-done((bf16[3,128,384]{2,1,0:T(8,128)(2,1)}, bf16[3,128,384]{2,1,0:T(8,128)(2,1)S(1)}, u32[]{:S(2)}, u32[]{:S(2)}) %collective-permute-start.4) | collective-permute-done | bytes 294944 | tf_op jit(solution)/shard_map/ppermute | solution.py:288
  27.2 1.5 %collective-permute-start.8 = (bf16[2,2,128,384]{3,2,1,0:T(8,128)(2,1)S(1)}, bf16[2,2,128,384]{3,2,1,0:T(8,128)(2,1)S(1)}, u32[]{:S(2)}, u32[]{:S(2)}) collective-permute-start(bf16[2,2,128,384]{3,2,1,0:T(8,128)(2,1)S(1)} %pad_maximum_fusion.2), channel_id=1, source_target_pairs={{0,1},{1,0},{2,3},{3,2},{4,5},{5,4},{6,7},{7,6},{8,9},{9,8},{10,11... | collective-permute-start | bytes 1179656 | tf_op jit(solution)/shard_map/ppermute | solution.py:296
  28.9 0.1 collective-permute-start.7
  29.0 0.0 copy-start.1
  29.0 0.0 copy-start
  29.1 0.6 collective-permute-start.6
  29.7 0.1 copy-done.1
  29.8 0.5 collective-permute-start
  30.3 1.6 %collective-permute-start.9 = (bf16[3,128,384]{2,1,0:T(8,128)(2,1)S(1)}, bf16[3,128,384]{2,1,0:T(8,128)(2,1)S(1)}, u32[]{:S(2)}, u32[]{:S(2)}) collective-permute-start(bf16[3,128,384]{2,1,0:T(8,128)(2,1)S(1)} %copy-done.4), channel_id=1, source_target_pairs={{0,2},{1,3},{2,0},{3,1},{4,6},{5,7},{6,4},{7,5},{8,10},{9,11},{10,... | collective-permute-start | bytes 884744 | tf_op jit(solution)/shard_map/ppermute | solution.py:288
  31.9 0.8 %collective-permute-start.10 = (bf16[3,128,384]{2,1,0:T(8,128)(2,1)S(1)}, bf16[3,128,384]{2,1,0:T(8,128)(2,1)S(1)}, u32[]{:S(2)}, u32[]{:S(2)}) collective-permute-start(bf16[3,128,384]{2,1,0:T(8,128)(2,1)S(1)} %copy-done.3), channel_id=1, source_target_pairs={{0,8},{1,9},{2,10},{3,11},{4,12},{5,13},{6,14},{7,15},{8,0},{9,1},... | collective-permute-start | bytes 884744 | tf_op jit(solution)/shard_map/ppermute | solution.py:288
  32.8 11.4 %shard_map.58 = (f32[6,16,128]{2,1,0:T(8,128)S(1)}, bf16[6,512,128]{2,1,0:T(8,128)(2,1)S(1)}, bf16[384,512]{1,0:T(8,128)(2,1)S(1)}, bf16[6,256,128]{2,1,0:T(8,12...) custom-call(s32[16]{0:T(128)S(1)} %copy-done.2, ...), custom_call_target="tpu_custom_call" | custom-call | tf_op jit(solution)/shard_map/pallas_call | solution.py:210
  44.3 1.0 %collective-permute-start.11 = (bf16[2,2,128,384]{3,2,1,0:T(8,128)(2,1)S(1)}, bf16[2,2,128,384]{3,2,1,0:T(8,128)(2,1)S(1)}, u32[]{:S(2)}, u32[]{:S(2)}) collective-permute-start(bf16[2,2,128,384]{3,2,1,0:T(8,128)(2,1)S(1)} %pad_maximum_fusion.3), channel_id=1, source_target_pairs={{0,1},{1,0},{2,3},{3,2},{4,5},{5,4},{6,7},{7,6},{8,9},{9,8},{10,11... | collective-permute-start | bytes 1179656 | tf_op jit(solution)/shard_map/ppermute | solution.py:296
  45.3 1.3 %collective-permute-done.11.refs_3_ = bf16[2,2,128,384]{3,2,1,0:T(8,128)(2,1)S(1)} collective-permute-done((bf16[2,2,128,384]{3,2,1,0:T(8,128)(2,1)S(1)}, bf16[2,2,128,384]{3,2,1,0:T(8,128)(2,1)S(1)}, u32[]{:S(2)}, u32[]{:S(2)}) %collective-permute-start.11) | collective-permute-done | bytes 393248 | tf_op jit(solution)/shard_map/ppermute | solution.py:296
  46.6 8.0 %shard_map.59 = bf16[8,128,384]{2,1,0:T(8,128)(2,1)S(1)} custom-call(s32[16]{0:T(128)S(1)} %copy-done.2, f32[6,16,128]{2,1,0:T(8,128)S(1)} %get-tuple-element.35.refs_0_, bf16[3,128,384]{2,1,0:T(8,128)(2,1)S(1)} %collective-permute-done.9.refs_1_, bf16[3,128,384]{2,1,0:T(8,128)(2,1)S(1)} %collective-permute-done.10.refs_2_, ...), custom_call_target="tpu_custom_call" | custom-call | tf_op jit(solution)/shard_map/pallas_call | solution.py:210
  54.6 16.0 %all_to_all.5.blocks_ref = bf16[8,128,384]{2,1,0:T(8,128)(2,1)} all-to-all(bf16[8,128,384]{2,1,0:T(8,128)(2,1)S(1)} %shard_map.59), channel_id=1, replica_groups={{0,2,4,6,8,10,12,14},{1,3,5,7,9,11,13,15},{16,18,20,22,24,26,28,30},{17..., dimensions={0} | all-to-all | bytes 1572864 | tf_op jit(solution)/shard_map/all_to_all | solution.py:304
  70.6 2.1 %shard_map.60 = bf16[1,128,3072]{2,1,0:T(8,128)(2,1)} custom-call(bf16[8,128,384]{2,1,0:T(8,128)(2,1)} %all_to_all.5.blocks_ref), custom_call_target="tpu_custom_call" | custom-call | tf_op jit(solution)/shard_map/pallas_call | solution.py:267
  (28 shorter events, 0.4 us)
Async XLA Ops:
  1.8 16.0 %collective-permute-start.5 = (bf16[3,128,384]{2,1,0:T(8,128)(2,1)}, bf16[3,128,384]{2,1,0:T(8,128)(2,1)S(1)}, u32[]{:S(2)}, u32[]{:S(2)}) collective-permute-start(bf16[3,128,384]{2,1,0:T(8,128)(2,1)} %shard_map.57), channel_id=1, source_target_pairs={{0,10},{1,11},{2,8},{3,9},{4,14},{5,15},{6,12},{7,13},{8,2},{9,3},... | collective-permute-start | bytes 884744 | tf_op jit(solution)/shard_map/ppermute | solution.py:288
  9.5 19.5 %collective-permute-start.1 = (bf16[3,128,384]{2,1,0:T(8,128)(2,1)}, bf16[3,128,384]{2,1,0:T(8,128)(2,1)S(1)}, u32[]{:S(2)}, u32[]{:S(2)}) collective-permute-start(bf16[3,128,384]{2,1,0:T(8,128)(2,1)} %get-tuple-element.31), channel_id=1, source_target_pairs={{0,4},{1,5},{2,6},{3,7},{4,8},{5,9},{6,10},{7,11},{8,12},{9,13},{1... | collective-permute-start | bytes 884744 | tf_op jit(solution)/shard_map/ppermute | solution.py:288
  9.9 18.8 %collective-permute-start.2 = (bf16[3,128,384]{2,1,0:T(8,128)(2,1)}, bf16[3,128,384]{2,1,0:T(8,128)(2,1)S(1)}, u32[]{:S(2)}, u32[]{:S(2)}) collective-permute-start(bf16[3,128,384]{2,1,0:T(8,128)(2,1)} %get-tuple-element.32), channel_id=1, source_target_pairs={{0,6},{1,7},{2,4},{3,5},{4,10},{5,11},{6,8},{7,9},{8,14},{9,15},{1... | collective-permute-start | bytes 884744 | tf_op jit(solution)/shard_map/ppermute | solution.py:288
  10.0 18.8 %collective-permute-start.3 = (bf16[3,128,384]{2,1,0:T(8,128)(2,1)}, bf16[3,128,384]{2,1,0:T(8,128)(2,1)S(1)}, u32[]{:S(2)}, u32[]{:S(2)}) collective-permute-start(bf16[3,128,384]{2,1,0:T(8,128)(2,1)} %get-tuple-element.33), channel_id=1, source_target_pairs={{0,12},{1,13},{2,14},{3,15},{4,0},{5,1},{6,2},{7,3},{8,4},{9,5},{1... | collective-permute-start | bytes 884744 | tf_op jit(solution)/shard_map/ppermute | solution.py:288
  12.2 14.9 %collective-permute-start.4 = (bf16[3,128,384]{2,1,0:T(8,128)(2,1)}, bf16[3,128,384]{2,1,0:T(8,128)(2,1)S(1)}, u32[]{:S(2)}, u32[]{:S(2)}) collective-permute-start(bf16[3,128,384]{2,1,0:T(8,128)(2,1)} %get-tuple-element.34), channel_id=1, source_target_pairs={{0,14},{1,15},{2,12},{3,13},{4,2},{5,3},{6,0},{7,1},{8,6},{9,7},{1... | collective-permute-start | bytes 884744 | tf_op jit(solution)/shard_map/ppermute | solution.py:288
  27.2 5.5 %collective-permute-start.8 = (bf16[2,2,128,384]{3,2,1,0:T(8,128)(2,1)S(1)}, bf16[2,2,128,384]{3,2,1,0:T(8,128)(2,1)S(1)}, u32[]{:S(2)}, u32[]{:S(2)}) collective-permute-start(bf16[2,2,128,384]{3,2,1,0:T(8,128)(2,1)S(1)} %pad_maximum_fusion.2), channel_id=1, source_target_pairs={{0,1},{1,0},{2,3},{3,2},{4,5},{5,4},{6,7},{7,6},{8,9},{9,8},{10,11... | collective-permute-start | bytes 1179656 | tf_op jit(solution)/shard_map/ppermute | solution.py:296
  28.9 3.9 %collective-permute-start.7 = (bf16[2,2,128,384]{3,2,1,0:T(8,128)(2,1)S(1)}, bf16[2,2,128,384]{3,2,1,0:T(8,128)(2,1)S(1)}, u32[]{:S(2)}, u32[]{:S(2)}) collective-permute-start(bf16[2,2,128,384]{3,2,1,0:T(8,128)(2,1)S(1)} %pad_maximum_fusion.1), channel_id=1, source_target_pairs={{0,1},{1,0},{2,3},{3,2},{4,5},{5,4},{6,7},{7,6},{8,9},{9,8},{10,11... | collective-permute-start | bytes 1179656 | tf_op jit(solution)/shard_map/ppermute | solution.py:296
  29.0 1.3 %copy-start.4 = (bf16[3,128,384]{2,1,0:T(8,128)(2,1)S(1)}, bf16[3,128,384]{2,1,0:T(8,128)(2,1)}, u32[]{:S(2)}) copy-start(bf16[3,128,384]{2,1,0:T(8,128)(2,1)} %get-tuple-element.36) | copy-start | bytes 884740
  29.0 0.8 %copy-start.1 = (s32[1,3,16,16]{3,2,1,0:T(8,128)S(1)}, s32[1,3,16,16]{3,2,1,0:T(8,128)}, u32[]{:S(2)}) copy-start(s32[1,3,16,16]{3,2,1,0:T(8,128)} %refs_0_.1) | copy-start | bytes 9220
  29.0 2.9 %copy-start.3 = (bf16[3,128,384]{2,1,0:T(8,128)(2,1)S(1)}, bf16[3,128,384]{2,1,0:T(8,128)(2,1)}, u32[]{:S(2)}) copy-start(bf16[3,128,384]{2,1,0:T(8,128)(2,1)} %get-tuple-element.37) | copy-start | bytes 884740
  29.0 3.7 %copy-start = (bf16[3,128,384]{2,1,0:T(8,128)(2,1)S(1)}, bf16[3,128,384]{2,1,0:T(8,128)(2,1)}, u32[]{:S(2)}) copy-start(bf16[3,128,384]{2,1,0:T(8,128)(2,1)} %get-tuple-element.30.refs_2_) | copy-start | bytes 884740
  29.1 3.6 %collective-permute-start.6 = (bf16[2,2,128,384]{3,2,1,0:T(8,128)(2,1)S(1)}, bf16[2,2,128,384]{3,2,1,0:T(8,128)(2,1)S(1)}, u32[]{:S(2)}, u32[]{:S(2)}) collective-permute-start(bf16[2,2,128,384]{3,2,1,0:T(8,128)(2,1)S(1)} %pad_maximum_fusion), channel_id=1, source_target_pairs={{0,1},{1,0},{2,3},{3,2},{4,5},{5,4},{6,7},{7,6},{8,9},{9,8},{10,11... | collective-permute-start | bytes 1179656 | tf_op jit(solution)/shard_map/ppermute | solution.py:296
  29.8 2.1 %collective-permute-start = (s32[1,3,16,16]{3,2,1,0:T(8,128)S(1)}, s32[1,3,16,16]{3,2,1,0:T(8,128)S(1)}, u32[]{:S(2)}, u32[]{:S(2)}) collective-permute-start(s32[1,3,16,16]{3,2,1,0:T(8,128)S(1)} %copy-done.1), channel_id=1, source_target_pairs={{0,1},{1,0},{2,3},{3,2},{4,5},{5,4},{6,7},{7,6},{8,9},{9,8},{10,11... | collective-permute-start | bytes 9224 | tf_op jit(solution)/shard_map/ppermute | solution.py:281
  30.3 2.5 %copy-start.2 = (s32[16]{0:T(128)S(1)}, s32[16]{0:T(128)}, u32[]{:S(2)}) copy-start(s32[16]{0:T(128)} %lengths_ref.3) | copy-start | bytes 196
  30.3 13.9 %collective-permute-start.9 = (bf16[3,128,384]{2,1,0:T(8,128)(2,1)S(1)}, bf16[3,128,384]{2,1,0:T(8,128)(2,1)S(1)}, u32[]{:S(2)}, u32[]{:S(2)}) collective-permute-start(bf16[3,128,384]{2,1,0:T(8,128)(2,1)S(1)} %copy-done.4), channel_id=1, source_target_pairs={{0,2},{1,3},{2,0},{3,1},{4,6},{5,7},{6,4},{7,5},{8,10},{9,11},{10,... | collective-permute-start | bytes 884744 | tf_op jit(solution)/shard_map/ppermute | solution.py:288
  31.9 12.2 %collective-permute-start.10 = (bf16[3,128,384]{2,1,0:T(8,128)(2,1)S(1)}, bf16[3,128,384]{2,1,0:T(8,128)(2,1)S(1)}, u32[]{:S(2)}, u32[]{:S(2)}) collective-permute-start(bf16[3,128,384]{2,1,0:T(8,128)(2,1)S(1)} %copy-done.3), channel_id=1, source_target_pairs={{0,8},{1,9},{2,10},{3,11},{4,12},{5,13},{6,14},{7,15},{8,0},{9,1},... | collective-permute-start | bytes 884744 | tf_op jit(solution)/shard_map/ppermute | solution.py:288
  44.3 2.4 %collective-permute-start.11 = (bf16[2,2,128,384]{3,2,1,0:T(8,128)(2,1)S(1)}, bf16[2,2,128,384]{3,2,1,0:T(8,128)(2,1)S(1)}, u32[]{:S(2)}, u32[]{:S(2)}) collective-permute-start(bf16[2,2,128,384]{3,2,1,0:T(8,128)(2,1)S(1)} %pad_maximum_fusion.3), channel_id=1, source_target_pairs={{0,1},{1,0},{2,3},{3,2},{4,5},{5,4},{6,7},{7,6},{8,9},{9,8},{10,11... | collective-permute-start | bytes 1179656 | tf_op jit(solution)/shard_map/ppermute | solution.py:296

commit v5 on v4

--- a/solution.py
+++ b/solution.py
@@ -113,10 +113,7 @@
     queries = [group[2] for group in old + made]
 
     every = tuple(range(seen + len(new)))
-    items = []
-    if seen:
-        items += [(head, [(u, new) for u in range(seen)]) for head in range(2)]
-    items += [(head, [(u, every)]) for u in new for head in range(2)]
+    items = [(head, [(u, new) for u in range(seen)] + [(u, every) for u in new]) for head in range(2)]
 
     def chunks(item):
         return [(u, group, part) for u, groups in item[1] for group in groups for part in range(KB // CK)]
@@ -130,7 +127,7 @@
         top = jnp.max(s.reshape(CK // 8, 8, QB), axis=0)
         return {**tops, u: jnp.maximum(tops[u], top) if u in tops else top}
 
-    def one_pair(pair, tops):
+    def one_pair(pair, tops, ends=False):
         finished = {}
         columns = pl.ds(pl.multiple_of(pair * PAIR, PAIR), PAIR)
         for index, item in enumerate(items):
@@ -150,8 +147,8 @@
                     total[u] = jnp.where(lax.broadcasted_iota(jnp.int32, (8, QB), 0) == 0, faded, 0.0)
             now = chunks(item)
             following = (index + 1) % len(items)
-            next_pair = pair if following else jnp.minimum(pair + 1, PAIRS - 1)
-            later = len(chunks(items[following]))
+            next_pair = pair if following else pair + 1
+            later = 0 if ends and not following else len(chunks(items[following]))
             tops = {}
             done = 0
             for place, (u, group, part) in enumerate(now):
@@ -187,7 +184,8 @@
     tops = {}
     for place in range(len(chunks(items[0]))):
         tops = score_chunk(0, 0, place, tops)
-    lax.fori_loop(0, PAIRS, one_pair, tops)
+    tops = lax.fori_loop(0, PAIRS - 1, one_pair, tops)
+    one_pair(PAIRS - 1, tops, ends=True)
 
 
 def attend_wave(wave, lengths, masks, blocks, others, old):
@@ -199,7 +197,7 @@
     made = [((2 * PAIRS, 16, PAIR), f32)] if wave == 0 else []
     made += kept + [((PAIRS, 16, QB), f32), ((WIDTH, QB), f32)] * groups
     operands = (lengths, *masks, *blocks, *others, *[array for group in old for array in group])
-    scratch = [pltpu.VMEM((groups * KB, QB), f32)] * 2
+    scratch = [pltpu.VMEM(((new[0] * len(new) + len(new) * groups) * KB, QB), f32)] * 2
     if last:
         out_shape = jax.ShapeDtypeStruct((CHIPS, TILE, WIDTH), bf16)
         scratch = [pltpu.VMEM(*array) for array in made[: len(made) - 2 * groups]] + scratch

time: 73.5 us -> 69.9 us (0.951)
  Pallas kernels: 28 us -> 24.5 us
    pallas_call x2, Pallas kernels: 19.4 us -> 16 us  [attend_wave(): pl.pallas_call(functools.partial(wave_kernel, wave), out_shape=out_shape,...]
  transfers between devices with their start and end apart: 12 -> 12, of which waited for: 2 -> 2; matrix products, arithmetic and copies ran while one was open for 2% -> 2% of each run, Pallas kernels for 22% -> 20%
where the time goes in v5:
time: 69.9 us; the launch traced here: 69.2 us
  Pallas kernels  24.5 us (35%)
  starting transfers between devices  16.6 us (24%)
  blocking collectives  15.6 us (22%)
  waiting for transfers between devices  10.7 us (15%)
  local copies, waits for them, and re-layouts  1.25 us (2%)
    pallas_call x2, Pallas kernels, attend_wave(): pl.pallas_call(functools.partial(wave_kernel, wave), out_shape=out_shape,...  16 us
    all_to_all x1, blocking collectives, on_device(): back = lax.all_to_all(out, 'seq', 0, 0, tiled=True, axis_index_groups=every)  15.6 us
    ppermute x7, starting transfers between devices, on_device(): blocks.append(lax.ppermute(sent[slot], 'seq', route(*AWAY[slot])))  12.7 us
    ppermute x7, waiting for transfers between devices, on_device(): blocks.append(lax.ppermute(sent[slot], 'seq', route(*AWAY[slot])))  9.3 us
    pallas_call x3, Pallas kernels, split_columns(): pl.pallas_call(functools.partial(split_kernel, slots), out_shape=[jax.Sha...  6.51 us
    ppermute x4, starting transfers between devices, on_device(): lax.ppermute(jnp.stack([block[1:] for block in now[i:i + 2]]), 'seq', OTH...  3.4 us
    pallas_call x1, Pallas kernels, join_columns(): pl.pallas_call(join_kernel, out_shape=jax.ShapeDtypeStruct((1, TILE, CHIP...  2.07 us
  transfers between devices with their start and end apart: 12, of which 2 were waited for; matrix products, arithmetic and copies ran while one was open for 2% of the time, Pallas kernels for 20%

profile of v5, /device:TPU:1, one launch (start us, length us, event | category | flops | bytes accessed | tf_op | source)
XLA Modules:
  0.0 69.2 jit_solution(16828634218232727765)
XLA Ops:
  0.0 1.8 %shard_map.57 = bf16[3,128,384]{2,1,0:T(8,128)(2,1)} custom-call(bf16[1,128,3072]{2,1,0:T(8,128)(2,1)} %q_ref.5, bf16[1,128,3072]{2,1,0:T(8,128)(2,1)} %k_ref.5, bf16[1,128,3072]{2,1,0:T(8,128)(2,1)} %v_ref.5), custom_call_target="tpu_custom_call" | custom-call | tf_op jit(solution)/shard_map/pallas_call | solution.py:242
  1.8 5.2 %collective-permute-start.5 = (bf16[3,128,384]{2,1,0:T(8,128)(2,1)}, bf16[3,128,384]{2,1,0:T(8,128)(2,1)S(1)}, u32[]{:S(2)}, u32[]{:S(2)}) collective-permute-start(bf16[3,128,384]{2,1,0:T(8,128)(2,1)} %shard_map.57), channel_id=1, source_target_pairs={{0,10},{1,11},{2,8},{3,9},{4,14},{5,15},{6,12},{7,13},{8,2},{9,3},... | collective-permute-start | bytes 884744 | tf_op jit(solution)/shard_map/ppermute | solution.py:286
  6.9 2.5 %shard_map.56 = (bf16[3,128,384]{2,1,0:T(8,128)(2,1)}, bf16[3,128,384]{2,1,0:T(8,128)(2,1)}, bf16[3,128,384]{2,1,0:T(8,128)(2,1)}, bf16[3,128,384]{2,1,0:T(8,128)(2,1)}) custom-call(bf16[1,128,3072]{2,1,0:T(8,128)(2,1)} %q_ref.5, bf16[1,128,3072]{2,1,0:T(8,128)(2,1)} %k_ref.5, bf16[1,128,3072]{2,1,0:T(8,128)(2,1)} %v_ref.5), custom_call_target="tpu_custom_call" | custom-call | tf_op jit(solution)/shard_map/pallas_call | solution.py:242
  9.5 0.5 collective-permute-start.1
  10.0 2.3 %collective-permute-start.3 = (bf16[3,128,384]{2,1,0:T(8,128)(2,1)}, bf16[3,128,384]{2,1,0:T(8,128)(2,1)S(1)}, u32[]{:S(2)}, u32[]{:S(2)}) collective-permute-start(bf16[3,128,384]{2,1,0:T(8,128)(2,1)} %get-tuple-element.33), channel_id=1, source_target_pairs={{0,12},{1,13},{2,14},{3,15},{4,0},{5,1},{6,2},{7,3},{8,4},{9,5},{1... | collective-permute-start | bytes 884744 | tf_op jit(solution)/shard_map/ppermute | solution.py:286
  12.2 2.4 %collective-permute-start.4 = (bf16[3,128,384]{2,1,0:T(8,128)(2,1)}, bf16[3,128,384]{2,1,0:T(8,128)(2,1)S(1)}, u32[]{:S(2)}, u32[]{:S(2)}) collective-permute-start(bf16[3,128,384]{2,1,0:T(8,128)(2,1)} %get-tuple-element.34), channel_id=1, source_target_pairs={{0,14},{1,15},{2,12},{3,13},{4,2},{5,3},{6,0},{7,1},{8,6},{9,7},{1... | collective-permute-start | bytes 884744 | tf_op jit(solution)/shard_map/ppermute | solution.py:286
  14.6 2.2 %shard_map.55 = (bf16[3,128,384]{2,1,0:T(8,128)(2,1)}, bf16[3,128,384]{2,1,0:T(8,128)(2,1)}, bf16[3,128,384]{2,1,0:T(8,128)(2,1)}) custom-call(bf16[1,128,3072]{2,1,0:T(8,128)(2,1)} %q_ref.5, bf16[1,128,3072]{2,1,0:T(8,128)(2,1)} %k_ref.5, bf16[1,128,3072]{2,1,0:T(8,128)(2,1)} %v_ref.5), custom_call_target="tpu_custom_call" | custom-call | tf_op jit(solution)/shard_map/pallas_call | solution.py:242
  16.8 1.0 %slice_bitcast_fusion.7 = bf16[1,2,128,384]{3,2,1,0:T(8,128)(2,1)S(1)} fusion(bf16[3,128,384]{2,1,0:T(8,128)(2,1)} %get-tuple-element.30.refs_2_), kind=kLoop, calls=%fused_computation.11 | loop fusion | bytes 393216 | tf_op jit(solution)/shard_map/stack | solution.py:294
  17.8 9.3 %collective-permute-done.4.refs_6_ = bf16[3,128,384]{2,1,0:T(8,128)(2,1)S(1)} collective-permute-done((bf16[3,128,384]{2,1,0:T(8,128)(2,1)}, bf16[3,128,384]{2,1,0:T(8,128)(2,1)S(1)}, u32[]{:S(2)}, u32[]{:S(2)}) %collective-permute-start.4) | collective-permute-done | bytes 294944 | tf_op jit(solution)/shard_map/ppermute | solution.py:286
  27.2 1.5 %collective-permute-start.8 = (bf16[2,2,128,384]{3,2,1,0:T(8,128)(2,1)S(1)}, bf16[2,2,128,384]{3,2,1,0:T(8,128)(2,1)S(1)}, u32[]{:S(2)}, u32[]{:S(2)}) collective-permute-start(bf16[2,2,128,384]{3,2,1,0:T(8,128)(2,1)S(1)} %pad_maximum_fusion.2), channel_id=1, source_target_pairs={{0,1},{1,0},{2,3},{3,2},{4,5},{5,4},{6,7},{7,6},{8,9},{9,8},{10,11... | collective-permute-start | bytes 1179656 | tf_op jit(solution)/shard_map/ppermute | solution.py:294
  28.9 0.1 collective-permute-start.7
  29.0 0.0 copy-start.1
  29.0 0.0 copy-start
  29.1 0.6 collective-permute-start.6
  29.7 0.1 copy-done.1
  29.8 0.5 collective-permute-start
  30.3 1.6 %collective-permute-start.9 = (bf16[3,128,384]{2,1,0:T(8,128)(2,1)S(1)}, bf16[3,128,384]{2,1,0:T(8,128)(2,1)S(1)}, u32[]{:S(2)}, u32[]{:S(2)}) collective-permute-start(bf16[3,128,384]{2,1,0:T(8,128)(2,1)S(1)} %copy-done.4), channel_id=1, source_target_pairs={{0,2},{1,3},{2,0},{3,1},{4,6},{5,7},{6,4},{7,5},{8,10},{9,11},{10,... | collective-permute-start | bytes 884744 | tf_op jit(solution)/shard_map/ppermute | solution.py:286
  31.9 0.8 %collective-permute-start.10 = (bf16[3,128,384]{2,1,0:T(8,128)(2,1)S(1)}, bf16[3,128,384]{2,1,0:T(8,128)(2,1)S(1)}, u32[]{:S(2)}, u32[]{:S(2)}) collective-permute-start(bf16[3,128,384]{2,1,0:T(8,128)(2,1)S(1)} %copy-done.3), channel_id=1, source_target_pairs={{0,8},{1,9},{2,10},{3,11},{4,12},{5,13},{6,14},{7,15},{8,0},{9,1},... | collective-permute-start | bytes 884744 | tf_op jit(solution)/shard_map/ppermute | solution.py:286
  32.8 9.0 %shard_map.58 = (f32[6,16,128]{2,1,0:T(8,128)S(1)}, bf16[6,512,128]{2,1,0:T(8,128)(2,1)S(1)}, bf16[384,512]{1,0:T(8,128)(2,1)S(1)}, bf16[6,256,128]{2,1,0:T(8,12...) custom-call(s32[16]{0:T(128)S(1)} %copy-done.2, ...), custom_call_target="tpu_custom_call" | custom-call | tf_op jit(solution)/shard_map/pallas_call | solution.py:208
  41.9 1.2 %collective-permute-start.11 = (bf16[2,2,128,384]{3,2,1,0:T(8,128)(2,1)S(1)}, bf16[2,2,128,384]{3,2,1,0:T(8,128)(2,1)S(1)}, u32[]{:S(2)}, u32[]{:S(2)}) collective-permute-start(bf16[2,2,128,384]{3,2,1,0:T(8,128)(2,1)S(1)} %pad_maximum_fusion.3), channel_id=1, source_target_pairs={{0,1},{1,0},{2,3},{3,2},{4,5},{5,4},{6,7},{7,6},{8,9},{9,8},{10,11... | collective-permute-start | bytes 1179656 | tf_op jit(solution)/shard_map/ppermute | solution.py:294
  43.0 1.3 %collective-permute-done.11.refs_3_ = bf16[2,2,128,384]{3,2,1,0:T(8,128)(2,1)S(1)} collective-permute-done((bf16[2,2,128,384]{3,2,1,0:T(8,128)(2,1)S(1)}, bf16[2,2,128,384]{3,2,1,0:T(8,128)(2,1)S(1)}, u32[]{:S(2)}, u32[]{:S(2)}) %collective-permute-start.11) | collective-permute-done | bytes 393248 | tf_op jit(solution)/shard_map/ppermute | solution.py:294
  44.4 7.0 %shard_map.59 = bf16[8,128,384]{2,1,0:T(8,128)(2,1)S(1)} custom-call(s32[16]{0:T(128)S(1)} %copy-done.2, f32[6,16,128]{2,1,0:T(8,128)S(1)} %get-tuple-element.35.refs_0_, bf16[3,128,384]{2,1,0:T(8,128)(2,1)S(1)} %collective-permute-done.9.refs_1_, bf16[3,128,384]{2,1,0:T(8,128)(2,1)S(1)} %collective-permute-done.10.refs_2_, ...), custom_call_target="tpu_custom_call" | custom-call | tf_op jit(solution)/shard_map/pallas_call | solution.py:208
  51.4 15.6 %all_to_all.5.blocks_ref = bf16[8,128,384]{2,1,0:T(8,128)(2,1)} all-to-all(bf16[8,128,384]{2,1,0:T(8,128)(2,1)S(1)} %shard_map.59), channel_id=1, replica_groups={{0,2,4,6,8,10,12,14},{1,3,5,7,9,11,13,15},{16,18,20,22,24,26,28,30},{17..., dimensions={0} | all-to-all | bytes 1572864 | tf_op jit(solution)/shard_map/all_to_all | solution.py:302
  67.0 2.1 %shard_map.60 = bf16[1,128,3072]{2,1,0:T(8,128)(2,1)} custom-call(bf16[8,128,384]{2,1,0:T(8,128)(2,1)} %all_to_all.5.blocks_ref), custom_call_target="tpu_custom_call" | custom-call | tf_op jit(solution)/shard_map/pallas_call | solution.py:265
  (28 shorter events, 0.4 us)
Async XLA Ops:
  1.8 16.0 %collective-permute-start.5 = (bf16[3,128,384]{2,1,0:T(8,128)(2,1)}, bf16[3,128,384]{2,1,0:T(8,128)(2,1)S(1)}, u32[]{:S(2)}, u32[]{:S(2)}) collective-permute-start(bf16[3,128,384]{2,1,0:T(8,128)(2,1)} %shard_map.57), channel_id=1, source_target_pairs={{0,10},{1,11},{2,8},{3,9},{4,14},{5,15},{6,12},{7,13},{8,2},{9,3},... | collective-permute-start | bytes 884744 | tf_op jit(solution)/shard_map/ppermute | solution.py:286
  9.5 19.5 %collective-permute-start.1 = (bf16[3,128,384]{2,1,0:T(8,128)(2,1)}, bf16[3,128,384]{2,1,0:T(8,128)(2,1)S(1)}, u32[]{:S(2)}, u32[]{:S(2)}) collective-permute-start(bf16[3,128,384]{2,1,0:T(8,128)(2,1)} %get-tuple-element.31), channel_id=1, source_target_pairs={{0,4},{1,5},{2,6},{3,7},{4,8},{5,9},{6,10},{7,11},{8,12},{9,13},{1... | collective-permute-start | bytes 884744 | tf_op jit(solution)/shard_map/ppermute | solution.py:286
  9.9 18.8 %collective-permute-start.2 = (bf16[3,128,384]{2,1,0:T(8,128)(2,1)}, bf16[3,128,384]{2,1,0:T(8,128)(2,1)S(1)}, u32[]{:S(2)}, u32[]{:S(2)}) collective-permute-start(bf16[3,128,384]{2,1,0:T(8,128)(2,1)} %get-tuple-element.32), channel_id=1, source_target_pairs={{0,6},{1,7},{2,4},{3,5},{4,10},{5,11},{6,8},{7,9},{8,14},{9,15},{1... | collective-permute-start | bytes 884744 | tf_op jit(solution)/shard_map/ppermute | solution.py:286
  10.0 18.8 %collective-permute-start.3 = (bf16[3,128,384]{2,1,0:T(8,128)(2,1)}, bf16[3,128,384]{2,1,0:T(8,128)(2,1)S(1)}, u32[]{:S(2)}, u32[]{:S(2)}) collective-permute-start(bf16[3,128,384]{2,1,0:T(8,128)(2,1)} %get-tuple-element.33), channel_id=1, source_target_pairs={{0,12},{1,13},{2,14},{3,15},{4,0},{5,1},{6,2},{7,3},{8,4},{9,5},{1... | collective-permute-start | bytes 884744 | tf_op jit(solution)/shard_map/ppermute | solution.py:286
  12.2 14.9 %collective-permute-start.4 = (bf16[3,128,384]{2,1,0:T(8,128)(2,1)}, bf16[3,128,384]{2,1,0:T(8,128)(2,1)S(1)}, u32[]{:S(2)}, u32[]{:S(2)}) collective-permute-start(bf16[3,128,384]{2,1,0:T(8,128)(2,1)} %get-tuple-element.34), channel_id=1, source_target_pairs={{0,14},{1,15},{2,12},{3,13},{4,2},{5,3},{6,0},{7,1},{8,6},{9,7},{1... | collective-permute-start | bytes 884744 | tf_op jit(solution)/shard_map/ppermute | solution.py:286
  27.2 5.5 %collective-permute-start.8 = (bf16[2,2,128,384]{3,2,1,0:T(8,128)(2,1)S(1)}, bf16[2,2,128,384]{3,2,1,0:T(8,128)(2,1)S(1)}, u32[]{:S(2)}, u32[]{:S(2)}) collective-permute-start(bf16[2,2,128,384]{3,2,1,0:T(8,128)(2,1)S(1)} %pad_maximum_fusion.2), channel_id=1, source_target_pairs={{0,1},{1,0},{2,3},{3,2},{4,5},{5,4},{6,7},{7,6},{8,9},{9,8},{10,11... | collective-permute-start | bytes 1179656 | tf_op jit(solution)/shard_map/ppermute | solution.py:294
  28.9 3.9 %collective-permute-start.7 = (bf16[2,2,128,384]{3,2,1,0:T(8,128)(2,1)S(1)}, bf16[2,2,128,384]{3,2,1,0:T(8,128)(2,1)S(1)}, u32[]{:S(2)}, u32[]{:S(2)}) collective-permute-start(bf16[2,2,128,384]{3,2,1,0:T(8,128)(2,1)S(1)} %pad_maximum_fusion.1), channel_id=1, source_target_pairs={{0,1},{1,0},{2,3},{3,2},{4,5},{5,4},{6,7},{7,6},{8,9},{9,8},{10,11... | collective-permute-start | bytes 1179656 | tf_op jit(solution)/shard_map/ppermute | solution.py:294
  29.0 1.3 %copy-start.4 = (bf16[3,128,384]{2,1,0:T(8,128)(2,1)S(1)}, bf16[3,128,384]{2,1,0:T(8,128)(2,1)}, u32[]{:S(2)}) copy-start(bf16[3,128,384]{2,1,0:T(8,128)(2,1)} %get-tuple-element.36) | copy-start | bytes 884740
  29.0 0.8 %copy-start.1 = (s32[1,3,16,16]{3,2,1,0:T(8,128)S(1)}, s32[1,3,16,16]{3,2,1,0:T(8,128)}, u32[]{:S(2)}) copy-start(s32[1,3,16,16]{3,2,1,0:T(8,128)} %refs_0_.1) | copy-start | bytes 9220
  29.0 2.9 %copy-start.3 = (bf16[3,128,384]{2,1,0:T(8,128)(2,1)S(1)}, bf16[3,128,384]{2,1,0:T(8,128)(2,1)}, u32[]{:S(2)}) copy-start(bf16[3,128,384]{2,1,0:T(8,128)(2,1)} %get-tuple-element.37) | copy-start | bytes 884740
  29.0 3.7 %copy-start = (bf16[3,128,384]{2,1,0:T(8,128)(2,1)S(1)}, bf16[3,128,384]{2,1,0:T(8,128)(2,1)}, u32[]{:S(2)}) copy-start(bf16[3,128,384]{2,1,0:T(8,128)(2,1)} %get-tuple-element.30.refs_2_) | copy-start | bytes 884740
  29.1 3.6 %collective-permute-start.6 = (bf16[2,2,128,384]{3,2,1,0:T(8,128)(2,1)S(1)}, bf16[2,2,128,384]{3,2,1,0:T(8,128)(2,1)S(1)}, u32[]{:S(2)}, u32[]{:S(2)}) collective-permute-start(bf16[2,2,128,384]{3,2,1,0:T(8,128)(2,1)S(1)} %pad_maximum_fusion), channel_id=1, source_target_pairs={{0,1},{1,0},{2,3},{3,2},{4,5},{5,4},{6,7},{7,6},{8,9},{9,8},{10,11... | collective-permute-start | bytes 1179656 | tf_op jit(solution)/shard_map/ppermute | solution.py:294
  29.8 2.1 %collective-permute-start = (s32[1,3,16,16]{3,2,1,0:T(8,128)S(1)}, s32[1,3,16,16]{3,2,1,0:T(8,128)S(1)}, u32[]{:S(2)}, u32[]{:S(2)}) collective-permute-start(s32[1,3,16,16]{3,2,1,0:T(8,128)S(1)} %copy-done.1), channel_id=1, source_target_pairs={{0,1},{1,0},{2,3},{3,2},{4,5},{5,4},{6,7},{7,6},{8,9},{9,8},{10,11... | collective-permute-start | bytes 9224 | tf_op jit(solution)/shard_map/ppermute | solution.py:279
  30.3 2.5 %copy-start.2 = (s32[16]{0:T(128)S(1)}, s32[16]{0:T(128)}, u32[]{:S(2)}) copy-start(s32[16]{0:T(128)} %lengths_ref.3) | copy-start | bytes 196
  30.3 11.5 %collective-permute-start.9 = (bf16[3,128,384]{2,1,0:T(8,128)(2,1)S(1)}, bf16[3,128,384]{2,1,0:T(8,128)(2,1)S(1)}, u32[]{:S(2)}, u32[]{:S(2)}) collective-permute-start(bf16[3,128,384]{2,1,0:T(8,128)(2,1)S(1)} %copy-done.4), channel_id=1, source_target_pairs={{0,2},{1,3},{2,0},{3,1},{4,6},{5,7},{6,4},{7,5},{8,10},{9,11},{10,... | collective-permute-start | bytes 884744 | tf_op jit(solution)/shard_map/ppermute | solution.py:286
  31.9 9.8 %collective-permute-start.10 = (bf16[3,128,384]{2,1,0:T(8,128)(2,1)S(1)}, bf16[3,128,384]{2,1,0:T(8,128)(2,1)S(1)}, u32[]{:S(2)}, u32[]{:S(2)}) collective-permute-start(bf16[3,128,384]{2,1,0:T(8,128)(2,1)S(1)} %copy-done.3), channel_id=1, source_target_pairs={{0,8},{1,9},{2,10},{3,11},{4,12},{5,13},{6,14},{7,15},{8,0},{9,1},... | collective-permute-start | bytes 884744 | tf_op jit(solution)/shard_map/ppermute | solution.py:286
  41.9 2.5 %collective-permute-start.11 = (bf16[2,2,128,384]{3,2,1,0:T(8,128)(2,1)S(1)}, bf16[2,2,128,384]{3,2,1,0:T(8,128)(2,1)S(1)}, u32[]{:S(2)}, u32[]{:S(2)}) collective-permute-start(bf16[2,2,128,384]{3,2,1,0:T(8,128)(2,1)S(1)} %pad_maximum_fusion.3), channel_id=1, source_target_pairs={{0,1},{1,0},{2,3},{3,2},{4,5},{5,4},{6,7},{7,6},{8,9},{9,8},{10,11... | collective-permute-start | bytes 1179656 | tf_op jit(solution)/shard_map/ppermute | solution.py:294

commit v6 on v5

--- a/solution.py
+++ b/solution.py
@@ -14,7 +14,7 @@
 WIDTH = PAIRS * PAIR
 QB = 2 * TILE
 KB = 4 * TILE
-CK = 256
+CK = 512
 MASKED = -1e30
 SCALE = 0.125 * 1.4426950408889634
 

time: 69.9 us -> 69.8 us (level)
  no operation moved by 1% of the time
where the time goes in v6:
time: 69.8 us; the launch traced here: 69.1 us
  Pallas kernels  24.4 us (35%)
  starting transfers between devices  16.7 us (24%)
  blocking collectives  15.6 us (22%)
  waiting for transfers between devices  10.7 us (15%)
  local copies, waits for them, and re-layouts  1.25 us (2%)
    pallas_call x2, Pallas kernels, attend_wave(): pl.pallas_call(functools.partial(wave_kernel, wave), out_shape=out_shape,...  15.9 us
    all_to_all x1, blocking collectives, on_device(): back = lax.all_to_all(out, 'seq', 0, 0, tiled=True, axis_index_groups=every)  15.6 us
    ppermute x7, starting transfers between devices, on_device(): blocks.append(lax.ppermute(sent[slot], 'seq', route(*AWAY[slot])))  12.7 us
    ppermute x7, waiting for transfers between devices, on_device(): blocks.append(lax.ppermute(sent[slot], 'seq', route(*AWAY[slot])))  9.3 us
    pallas_call x3, Pallas kernels, split_columns(): pl.pallas_call(functools.partial(split_kernel, slots), out_shape=[jax.Sha...  6.51 us
    ppermute x4, starting transfers between devices, on_device(): lax.ppermute(jnp.stack([block[1:] for block in now[i:i + 2]]), 'seq', OTH...  3.45 us
    pallas_call x1, Pallas kernels, join_columns(): pl.pallas_call(join_kernel, out_shape=jax.ShapeDtypeStruct((1, TILE, CHIP...  2.07 us
  transfers between devices with their start and end apart: 12, of which 2 were waited for; matrix products, arithmetic and copies ran while one was open for 2% of the time, Pallas kernels for 20%

profile of v6, /device:TPU:1, one launch (start us, length us, event | category | flops | bytes accessed | tf_op | source)
XLA Modules:
  0.0 69.1 jit_solution(4246696336741172846)
XLA Ops:
  0.0 1.8 %shard_map.57 = bf16[3,128,384]{2,1,0:T(8,128)(2,1)} custom-call(bf16[1,128,3072]{2,1,0:T(8,128)(2,1)} %q_ref.5, bf16[1,128,3072]{2,1,0:T(8,128)(2,1)} %k_ref.5, bf16[1,128,3072]{2,1,0:T(8,128)(2,1)} %v_ref.5), custom_call_target="tpu_custom_call" | custom-call | tf_op jit(solution)/shard_map/pallas_call | solution.py:242
  1.8 5.2 %collective-permute-start.5 = (bf16[3,128,384]{2,1,0:T(8,128)(2,1)}, bf16[3,128,384]{2,1,0:T(8,128)(2,1)S(1)}, u32[]{:S(2)}, u32[]{:S(2)}) collective-permute-start(bf16[3,128,384]{2,1,0:T(8,128)(2,1)} %shard_map.57), channel_id=1, source_target_pairs={{0,10},{1,11},{2,8},{3,9},{4,14},{5,15},{6,12},{7,13},{8,2},{9,3},... | collective-permute-start | bytes 884744 | tf_op jit(solution)/shard_map/ppermute | solution.py:286
  6.9 2.5 %shard_map.56 = (bf16[3,128,384]{2,1,0:T(8,128)(2,1)}, bf16[3,128,384]{2,1,0:T(8,128)(2,1)}, bf16[3,128,384]{2,1,0:T(8,128)(2,1)}, bf16[3,128,384]{2,1,0:T(8,128)(2,1)}) custom-call(bf16[1,128,3072]{2,1,0:T(8,128)(2,1)} %q_ref.5, bf16[1,128,3072]{2,1,0:T(8,128)(2,1)} %k_ref.5, bf16[1,128,3072]{2,1,0:T(8,128)(2,1)} %v_ref.5), custom_call_target="tpu_custom_call" | custom-call | tf_op jit(solution)/shard_map/pallas_call | solution.py:242
  9.5 0.5 collective-permute-start.1
  10.0 2.3 %collective-permute-start.3 = (bf16[3,128,384]{2,1,0:T(8,128)(2,1)}, bf16[3,128,384]{2,1,0:T(8,128)(2,1)S(1)}, u32[]{:S(2)}, u32[]{:S(2)}) collective-permute-start(bf16[3,128,384]{2,1,0:T(8,128)(2,1)} %get-tuple-element.33), channel_id=1, source_target_pairs={{0,12},{1,13},{2,14},{3,15},{4,0},{5,1},{6,2},{7,3},{8,4},{9,5},{1... | collective-permute-start | bytes 884744 | tf_op jit(solution)/shard_map/ppermute | solution.py:286
  12.2 2.4 %collective-permute-start.4 = (bf16[3,128,384]{2,1,0:T(8,128)(2,1)}, bf16[3,128,384]{2,1,0:T(8,128)(2,1)S(1)}, u32[]{:S(2)}, u32[]{:S(2)}) collective-permute-start(bf16[3,128,384]{2,1,0:T(8,128)(2,1)} %get-tuple-element.34), channel_id=1, source_target_pairs={{0,14},{1,15},{2,12},{3,13},{4,2},{5,3},{6,0},{7,1},{8,6},{9,7},{1... | collective-permute-start | bytes 884744 | tf_op jit(solution)/shard_map/ppermute | solution.py:286
  14.6 2.2 %shard_map.55 = (bf16[3,128,384]{2,1,0:T(8,128)(2,1)}, bf16[3,128,384]{2,1,0:T(8,128)(2,1)}, bf16[3,128,384]{2,1,0:T(8,128)(2,1)}) custom-call(bf16[1,128,3072]{2,1,0:T(8,128)(2,1)} %q_ref.5, bf16[1,128,3072]{2,1,0:T(8,128)(2,1)} %k_ref.5, bf16[1,128,3072]{2,1,0:T(8,128)(2,1)} %v_ref.5), custom_call_target="tpu_custom_call" | custom-call | tf_op jit(solution)/shard_map/pallas_call | solution.py:242
  16.8 1.0 %slice_bitcast_fusion.7 = bf16[1,2,128,384]{3,2,1,0:T(8,128)(2,1)S(1)} fusion(bf16[3,128,384]{2,1,0:T(8,128)(2,1)} %get-tuple-element.30.refs_2_), kind=kLoop, calls=%fused_computation.11 | loop fusion | bytes 393216 | tf_op jit(solution)/shard_map/stack | solution.py:294
  17.8 9.3 %collective-permute-done.4.refs_6_ = bf16[3,128,384]{2,1,0:T(8,128)(2,1)S(1)} collective-permute-done((bf16[3,128,384]{2,1,0:T(8,128)(2,1)}, bf16[3,128,384]{2,1,0:T(8,128)(2,1)S(1)}, u32[]{:S(2)}, u32[]{:S(2)}) %collective-permute-start.4) | collective-permute-done | bytes 294944 | tf_op jit(solution)/shard_map/ppermute | solution.py:286
  27.2 1.5 %collective-permute-start.8 = (bf16[2,2,128,384]{3,2,1,0:T(8,128)(2,1)S(1)}, bf16[2,2,128,384]{3,2,1,0:T(8,128)(2,1)S(1)}, u32[]{:S(2)}, u32[]{:S(2)}) collective-permute-start(bf16[2,2,128,384]{3,2,1,0:T(8,128)(2,1)S(1)} %pad_maximum_fusion.2), channel_id=1, source_target_pairs={{0,1},{1,0},{2,3},{3,2},{4,5},{5,4},{6,7},{7,6},{8,9},{9,8},{10,11... | collective-permute-start | bytes 1179656 | tf_op jit(solution)/shard_map/ppermute | solution.py:294
  28.9 0.1 collective-permute-start.7
  29.0 0.0 copy-start.1
  29.0 0.0 copy-start
  29.1 0.6 collective-permute-start.6
  29.7 0.1 copy-done.1
  29.8 0.5 collective-permute-start
  30.3 1.6 %collective-permute-start.9 = (bf16[3,128,384]{2,1,0:T(8,128)(2,1)S(1)}, bf16[3,128,384]{2,1,0:T(8,128)(2,1)S(1)}, u32[]{:S(2)}, u32[]{:S(2)}) collective-permute-start(bf16[3,128,384]{2,1,0:T(8,128)(2,1)S(1)} %copy-done.4), channel_id=1, source_target_pairs={{0,2},{1,3},{2,0},{3,1},{4,6},{5,7},{6,4},{7,5},{8,10},{9,11},{10,... | collective-permute-start | bytes 884744 | tf_op jit(solution)/shard_map/ppermute | solution.py:286
  31.9 0.8 %collective-permute-start.10 = (bf16[3,128,384]{2,1,0:T(8,128)(2,1)S(1)}, bf16[3,128,384]{2,1,0:T(8,128)(2,1)S(1)}, u32[]{:S(2)}, u32[]{:S(2)}) collective-permute-start(bf16[3,128,384]{2,1,0:T(8,128)(2,1)S(1)} %copy-done.3), channel_id=1, source_target_pairs={{0,8},{1,9},{2,10},{3,11},{4,12},{5,13},{6,14},{7,15},{8,0},{9,1},... | collective-permute-start | bytes 884744 | tf_op jit(solution)/shard_map/ppermute | solution.py:286
  32.8 8.9 %shard_map.58 = (f32[6,16,128]{2,1,0:T(8,128)S(1)}, bf16[6,512,128]{2,1,0:T(8,128)(2,1)S(1)}, bf16[384,512]{1,0:T(8,128)(2,1)S(1)}, bf16[6,256,128]{2,1,0:T(8,12...) custom-call(s32[16]{0:T(128)S(1)} %copy-done.2, ...), custom_call_target="tpu_custom_call" | custom-call | tf_op jit(solution)/shard_map/pallas_call | solution.py:208
  41.8 1.2 %collective-permute-start.11 = (bf16[2,2,128,384]{3,2,1,0:T(8,128)(2,1)S(1)}, bf16[2,2,128,384]{3,2,1,0:T(8,128)(2,1)S(1)}, u32[]{:S(2)}, u32[]{:S(2)}) collective-permute-start(bf16[2,2,128,384]{3,2,1,0:T(8,128)(2,1)S(1)} %pad_maximum_fusion.3), channel_id=1, source_target_pairs={{0,1},{1,0},{2,3},{3,2},{4,5},{5,4},{6,7},{7,6},{8,9},{9,8},{10,11... | collective-permute-start | bytes 1179656 | tf_op jit(solution)/shard_map/ppermute | solution.py:294
  43.0 1.3 %collective-permute-done.11.refs_3_ = bf16[2,2,128,384]{3,2,1,0:T(8,128)(2,1)S(1)} collective-permute-done((bf16[2,2,128,384]{3,2,1,0:T(8,128)(2,1)S(1)}, bf16[2,2,128,384]{3,2,1,0:T(8,128)(2,1)S(1)}, u32[]{:S(2)}, u32[]{:S(2)}) %collective-permute-start.11) | collective-permute-done | bytes 393248 | tf_op jit(solution)/shard_map/ppermute | solution.py:294
  44.4 6.9 %shard_map.59 = bf16[8,128,384]{2,1,0:T(8,128)(2,1)S(1)} custom-call(s32[16]{0:T(128)S(1)} %copy-done.2, f32[6,16,128]{2,1,0:T(8,128)S(1)} %get-tuple-element.35.refs_0_, bf16[3,128,384]{2,1,0:T(8,128)(2,1)S(1)} %collective-permute-done.9.refs_1_, bf16[3,128,384]{2,1,0:T(8,128)(2,1)S(1)} %collective-permute-done.10.refs_2_, ...), custom_call_target="tpu_custom_call" | custom-call | tf_op jit(solution)/shard_map/pallas_call | solution.py:208
  51.3 15.6 %all_to_all.5.blocks_ref = bf16[8,128,384]{2,1,0:T(8,128)(2,1)} all-to-all(bf16[8,128,384]{2,1,0:T(8,128)(2,1)S(1)} %shard_map.59), channel_id=1, replica_groups={{0,2,4,6,8,10,12,14},{1,3,5,7,9,11,13,15},{16,18,20,22,24,26,28,30},{17..., dimensions={0} | all-to-all | bytes 1572864 | tf_op jit(solution)/shard_map/all_to_all | solution.py:302
  66.9 2.1 %shard_map.60 = bf16[1,128,3072]{2,1,0:T(8,128)(2,1)} custom-call(bf16[8,128,384]{2,1,0:T(8,128)(2,1)} %all_to_all.5.blocks_ref), custom_call_target="tpu_custom_call" | custom-call | tf_op jit(solution)/shard_map/pallas_call | solution.py:265
  (28 shorter events, 0.4 us)
Async XLA Ops:
  1.8 16.0 %collective-permute-start.5 = (bf16[3,128,384]{2,1,0:T(8,128)(2,1)}, bf16[3,128,384]{2,1,0:T(8,128)(2,1)S(1)}, u32[]{:S(2)}, u32[]{:S(2)}) collective-permute-start(bf16[3,128,384]{2,1,0:T(8,128)(2,1)} %shard_map.57), channel_id=1, source_target_pairs={{0,10},{1,11},{2,8},{3,9},{4,14},{5,15},{6,12},{7,13},{8,2},{9,3},... | collective-permute-start | bytes 884744 | tf_op jit(solution)/shard_map/ppermute | solution.py:286
  9.5 19.5 %collective-permute-start.1 = (bf16[3,128,384]{2,1,0:T(8,128)(2,1)}, bf16[3,128,384]{2,1,0:T(8,128)(2,1)S(1)}, u32[]{:S(2)}, u32[]{:S(2)}) collective-permute-start(bf16[3,128,384]{2,1,0:T(8,128)(2,1)} %get-tuple-element.31), channel_id=1, source_target_pairs={{0,4},{1,5},{2,6},{3,7},{4,8},{5,9},{6,10},{7,11},{8,12},{9,13},{1... | collective-permute-start | bytes 884744 | tf_op jit(solution)/shard_map/ppermute | solution.py:286
  9.9 18.8 %collective-permute-start.2 = (bf16[3,128,384]{2,1,0:T(8,128)(2,1)}, bf16[3,128,384]{2,1,0:T(8,128)(2,1)S(1)}, u32[]{:S(2)}, u32[]{:S(2)}) collective-permute-start(bf16[3,128,384]{2,1,0:T(8,128)(2,1)} %get-tuple-element.32), channel_id=1, source_target_pairs={{0,6},{1,7},{2,4},{3,5},{4,10},{5,11},{6,8},{7,9},{8,14},{9,15},{1... | collective-permute-start | bytes 884744 | tf_op jit(solution)/shard_map/ppermute | solution.py:286
  10.0 18.8 %collective-permute-start.3 = (bf16[3,128,384]{2,1,0:T(8,128)(2,1)}, bf16[3,128,384]{2,1,0:T(8,128)(2,1)S(1)}, u32[]{:S(2)}, u32[]{:S(2)}) collective-permute-start(bf16[3,128,384]{2,1,0:T(8,128)(2,1)} %get-tuple-element.33), channel_id=1, source_target_pairs={{0,12},{1,13},{2,14},{3,15},{4,0},{5,1},{6,2},{7,3},{8,4},{9,5},{1... | collective-permute-start | bytes 884744 | tf_op jit(solution)/shard_map/ppermute | solution.py:286
  12.2 14.9 %collective-permute-start.4 = (bf16[3,128,384]{2,1,0:T(8,128)(2,1)}, bf16[3,128,384]{2,1,0:T(8,128)(2,1)S(1)}, u32[]{:S(2)}, u32[]{:S(2)}) collective-permute-start(bf16[3,128,384]{2,1,0:T(8,128)(2,1)} %get-tuple-element.34), channel_id=1, source_target_pairs={{0,14},{1,15},{2,12},{3,13},{4,2},{5,3},{6,0},{7,1},{8,6},{9,7},{1... | collective-permute-start | bytes 884744 | tf_op jit(solution)/shard_map/ppermute | solution.py:286
  27.2 5.5 %collective-permute-start.8 = (bf16[2,2,128,384]{3,2,1,0:T(8,128)(2,1)S(1)}, bf16[2,2,128,384]{3,2,1,0:T(8,128)(2,1)S(1)}, u32[]{:S(2)}, u32[]{:S(2)}) collective-permute-start(bf16[2,2,128,384]{3,2,1,0:T(8,128)(2,1)S(1)} %pad_maximum_fusion.2), channel_id=1, source_target_pairs={{0,1},{1,0},{2,3},{3,2},{4,5},{5,4},{6,7},{7,6},{8,9},{9,8},{10,11... | collective-permute-start | bytes 1179656 | tf_op jit(solution)/shard_map/ppermute | solution.py:294
  28.9 3.9 %collective-permute-start.7 = (bf16[2,2,128,384]{3,2,1,0:T(8,128)(2,1)S(1)}, bf16[2,2,128,384]{3,2,1,0:T(8,128)(2,1)S(1)}, u32[]{:S(2)}, u32[]{:S(2)}) collective-permute-start(bf16[2,2,128,384]{3,2,1,0:T(8,128)(2,1)S(1)} %pad_maximum_fusion.1), channel_id=1, source_target_pairs={{0,1},{1,0},{2,3},{3,2},{4,5},{5,4},{6,7},{7,6},{8,9},{9,8},{10,11... | collective-permute-start | bytes 1179656 | tf_op jit(solution)/shard_map/ppermute | solution.py:294
  29.0 1.3 %copy-start.4 = (bf16[3,128,384]{2,1,0:T(8,128)(2,1)S(1)}, bf16[3,128,384]{2,1,0:T(8,128)(2,1)}, u32[]{:S(2)}) copy-start(bf16[3,128,384]{2,1,0:T(8,128)(2,1)} %get-tuple-element.36) | copy-start | bytes 884740
  29.0 0.8 %copy-start.1 = (s32[1,3,16,16]{3,2,1,0:T(8,128)S(1)}, s32[1,3,16,16]{3,2,1,0:T(8,128)}, u32[]{:S(2)}) copy-start(s32[1,3,16,16]{3,2,1,0:T(8,128)} %refs_0_.1) | copy-start | bytes 9220
  29.0 2.9 %copy-start.3 = (bf16[3,128,384]{2,1,0:T(8,128)(2,1)S(1)}, bf16[3,128,384]{2,1,0:T(8,128)(2,1)}, u32[]{:S(2)}) copy-start(bf16[3,128,384]{2,1,0:T(8,128)(2,1)} %get-tuple-element.37) | copy-start | bytes 884740
  29.0 3.7 %copy-start = (bf16[3,128,384]{2,1,0:T(8,128)(2,1)S(1)}, bf16[3,128,384]{2,1,0:T(8,128)(2,1)}, u32[]{:S(2)}) copy-start(bf16[3,128,384]{2,1,0:T(8,128)(2,1)} %get-tuple-element.30.refs_2_) | copy-start | bytes 884740
  29.1 3.6 %collective-permute-start.6 = (bf16[2,2,128,384]{3,2,1,0:T(8,128)(2,1)S(1)}, bf16[2,2,128,384]{3,2,1,0:T(8,128)(2,1)S(1)}, u32[]{:S(2)}, u32[]{:S(2)}) collective-permute-start(bf16[2,2,128,384]{3,2,1,0:T(8,128)(2,1)S(1)} %pad_maximum_fusion), channel_id=1, source_target_pairs={{0,1},{1,0},{2,3},{3,2},{4,5},{5,4},{6,7},{7,6},{8,9},{9,8},{10,11... | collective-permute-start | bytes 1179656 | tf_op jit(solution)/shard_map/ppermute | solution.py:294
  29.8 2.1 %collective-permute-start = (s32[1,3,16,16]{3,2,1,0:T(8,128)S(1)}, s32[1,3,16,16]{3,2,1,0:T(8,128)S(1)}, u32[]{:S(2)}, u32[]{:S(2)}) collective-permute-start(s32[1,3,16,16]{3,2,1,0:T(8,128)S(1)} %copy-done.1), channel_id=1, source_target_pairs={{0,1},{1,0},{2,3},{3,2},{4,5},{5,4},{6,7},{7,6},{8,9},{9,8},{10,11... | collective-permute-start | bytes 9224 | tf_op jit(solution)/shard_map/ppermute | solution.py:279
  30.3 2.5 %copy-start.2 = (s32[16]{0:T(128)S(1)}, s32[16]{0:T(128)}, u32[]{:S(2)}) copy-start(s32[16]{0:T(128)} %lengths_ref.3) | copy-start | bytes 196
  30.3 11.4 %collective-permute-start.9 = (bf16[3,128,384]{2,1,0:T(8,128)(2,1)S(1)}, bf16[3,128,384]{2,1,0:T(8,128)(2,1)S(1)}, u32[]{:S(2)}, u32[]{:S(2)}) collective-permute-start(bf16[3,128,384]{2,1,0:T(8,128)(2,1)S(1)} %copy-done.4), channel_id=1, source_target_pairs={{0,2},{1,3},{2,0},{3,1},{4,6},{5,7},{6,4},{7,5},{8,10},{9,11},{10,... | collective-permute-start | bytes 884744 | tf_op jit(solution)/shard_map/ppermute | solution.py:286
  31.9 9.8 %collective-permute-start.10 = (bf16[3,128,384]{2,1,0:T(8,128)(2,1)S(1)}, bf16[3,128,384]{2,1,0:T(8,128)(2,1)S(1)}, u32[]{:S(2)}, u32[]{:S(2)}) collective-permute-start(bf16[3,128,384]{2,1,0:T(8,128)(2,1)S(1)} %copy-done.3), channel_id=1, source_target_pairs={{0,8},{1,9},{2,10},{3,11},{4,12},{5,13},{6,14},{7,15},{8,0},{9,1},... | collective-permute-start | bytes 884744 | tf_op jit(solution)/shard_map/ppermute | solution.py:286
  41.8 2.6 %collective-permute-start.11 = (bf16[2,2,128,384]{3,2,1,0:T(8,128)(2,1)S(1)}, bf16[2,2,128,384]{3,2,1,0:T(8,128)(2,1)S(1)}, u32[]{:S(2)}, u32[]{:S(2)}) collective-permute-start(bf16[2,2,128,384]{3,2,1,0:T(8,128)(2,1)S(1)} %pad_maximum_fusion.3), channel_id=1, source_target_pairs={{0,1},{1,0},{2,3},{3,2},{4,5},{5,4},{6,7},{7,6},{8,9},{9,8},{10,11... | collective-permute-start | bytes 1179656 | tf_op jit(solution)/shard_map/ppermute | solution.py:294
